TPU v7x, 32 devices: a whole 2x2x4 slice. The times are simulated.
32 devices in a mesh: fsdp: 4 (over z), ctx: 2 (over core), tp: 4 (over y, x).
Axes of the slice: x: 2, y: 2, z: 4, core: 2. Of those that a mesh axis runs over, the one named last changes fastest.
Arguments:
- layer_input: bfloat16 [4, 2048, 1024], P('fsdp', 'ctx', 'tp'), may hold values from -6 to 6
- segment_ids: int32 [4, 2048], P('fsdp', 'ctx'), may hold values from 0 to 21, as said below
- cotangent: bfloat16 [4, 2048, 1024], P('fsdp', 'ctx', 'tp'), may hold values from -6 to 6
- norm_gain: float32 [1024], P('tp'), may hold values from 0.1 to 1.9
- ema_damping: float32 [16, 1024], P(None, 'tp'), may hold values from 0.000125 to 0.06666667
- ema_eta: float32 [16, 1024], P(None, 'tp'), may hold values from -8 to 8
- query_gain: float32 [128], replicated, may hold values from -8 to 8
- key_gain: float32 [128], replicated, may hold values from -8 to 8
- ffn_gain: float32 [1024], P('tp'), may hold values from 0.1 to 1.9
- shared_weight: bfloat16 [1024, 128], P(('fsdp', 'ctx')), may hold values from -0.1875 to 0.1875
- value_weight: bfloat16 [1024, 2048], P(('fsdp', 'ctx'), 'tp'), may hold values from -0.1875 to 0.1875
- gate_weight: bfloat16 [1024, 2048], P(('fsdp', 'ctx'), 'tp'), may hold values from -0.1875 to 0.1875
- hidden_weight: bfloat16 [1024, 1024], P('tp', ('fsdp', 'ctx')), may hold values from -0.1875 to 0.1875
- attended_weight: bfloat16 [2048, 1024], P('tp', ('fsdp', 'ctx')), may hold values from -0.5 to 0.5
- update_weight: bfloat16 [1024, 1024], P('tp', ('fsdp', 'ctx')), may hold values from -0.1875 to 0.1875
- ffn_up_weight: bfloat16 [1024, 4096], P(('fsdp', 'ctx'), 'tp'), may hold values from -0.1875 to 0.1875
- ffn_down_weight: bfloat16 [4096, 1024], P('tp', ('fsdp', 'ctx')), may hold values from -0.09375 to 0.09375
Outputs:
- layer_output: bfloat16 [4, 2048, 1024], P('fsdp', 'ctx', 'tp')
- grad_input: float32 [4, 2048, 1024], P('fsdp', 'ctx', 'tp')
- grad_norm_gain: float32 [1024], P('tp')
- grad_ema_damping: float32 [16, 1024], P(None, 'tp')
- grad_ema_eta: float32 [16, 1024], P(None, 'tp')
- grad_query_gain: float32 [128], replicated
- grad_key_gain: float32 [128], replicated
- grad_ffn_gain: float32 [1024], P('tp')
- grad_shared_weight: float32 [1024, 128], P(('fsdp', 'ctx'))
- grad_value_weight: float32 [1024, 2048], P(('fsdp', 'ctx'), 'tp')
- grad_gate_weight: float32 [1024, 2048], P(('fsdp', 'ctx'), 'tp')
- grad_hidden_weight: float32 [1024, 1024], P('tp', ('fsdp', 'ctx'))
- grad_attended_weight: float32 [2048, 1024], P('tp', ('fsdp', 'ctx'))
- grad_update_weight: float32 [1024, 1024], P('tp', ('fsdp', 'ctx'))
- grad_ffn_up_weight: float32 [1024, 4096], P(('fsdp', 'ctx'), 'tp')
- grad_ffn_down_weight: float32 [4096, 1024], P('tp', ('fsdp', 'ctx'))
Inputs may be any that keep to these rules, and one draw needn't show every extreme that they name: `segment_ids`: within each sequence the ids start at 0 at its first token, never fall and rise by at most one from a token to the next. Every document has 60 to 800 tokens, except that the last one of a sequence may be cut short; the first document of every sequence has exactly min(800, 2048) tokens, and in the 0th sequence every later document has exactly 60 tokens (cut short at its end).
All inputs are finite; a program needn't handle non-finite values.
Results may differ from a plain program's by a relative error of at most 0.015.
The roundings to bfloat16 on the way count: a program that leaves them out, or rounds other values in their place, can miss the bound.
Values may be sent and summed in bfloat16 or wider, within the bound.
A program may use at most 320 MiB of HBM per device.

v0:
```python
import math

import jax
import jax.numpy as jnp
from jax import lax
from jax.sharding import PartitionSpec as P

D = 1024
Z = 128


EPSILON = 1e-06


def prefix(array, axis, combine, identity):
    count, mine = (lax.axis_size(axis), lax.axis_index(axis))
    everything = jax.tree.map(lambda part: lax.all_gather(part, axis), array)
    start = jax.tree.map(
        lambda part, zero: jnp.broadcast_to(jnp.asarray(zero, part.dtype), part.shape),
        array,
        identity,
    )

    def lap(k, before):
        reached = k < mine
        new = combine(before, jax.tree.map(lambda part: part[k], everything))
        return jax.tree.map(lambda a, b: jnp.where(reached, a, b), new, before)

    return lax.fori_loop(0, count, lap, start)


def entering(array, axis, join, neutral):
    count = lax.axis_size(axis)
    place = lax.axis_index(axis)
    ahead = count - 1 - place
    gathered = jax.tree.map(
        lambda a, kind: lax.all_gather(a.astype(kind), axis), array, (jnp.bfloat16, jnp.bfloat16)
    )
    state = jax.tree.map(lambda a, e: jnp.zeros_like(a) + jnp.asarray(e, a.dtype), array, neutral)

    def one(lap, state):
        source = count - 1 - lap
        return join(
            state,
            jax.tree.map(
                lambda a, own: lax.dynamic_index_in_dim(a, source, 0, False).astype(own.dtype),
                gathered,
                array,
            ),
        )

    return lax.fori_loop(0, ahead, one, state)


def linear_pair(first_pair, second_pair):
    return (second_pair[0] * first_pair[0], second_pair[1] + second_pair[0] * first_pair[1])


def multiply(left_side, right_side):
    return jnp.dot(left_side, right_side, preferred_element_type=jnp.float32)


def multiply_left(left_side, right_side):
    return lax.dot_general(
        left_side, right_side, (((0,), (0,)), ((), ())), preferred_element_type=jnp.float32
    )


def multiply_right(left_side, right_side):
    return lax.dot_general(
        left_side, right_side, (((1,), (1,)), ((), ())), preferred_element_type=jnp.float32
    )


def silu_grad(pre_act):
    sigmoid_pre = jax.nn.sigmoid(pre_act)
    return sigmoid_pre * (1.0 + pre_act * (1.0 - sigmoid_pre))


def feature_total(row_values):
    return lax.psum(row_values, "tp")


def gather_features(stacked):
    return lax.all_gather(stacked, "tp", axis=2, tiled=True)


def sum_features(stacked):
    return lax.psum_scatter(stacked, "tp", scatter_dimension=2, tiled=True)


def gather_grads(stacked):
    return lax.all_gather(stacked, "tp", axis=2, tiled=True)


def sum_grads(stacked):
    return lax.psum_scatter(stacked, "tp", scatter_dimension=2, tiled=True)


def gather_weights(
    shared_weight,
    value_weight,
    gate_weight,
    hidden_weight,
    attended_weight,
    update_weight,
    ffn_up_weight,
    ffn_down_weight,
):
    return (
        lax.all_gather(shared_weight, ("fsdp", "ctx"), axis=0, tiled=True),
        lax.all_gather(value_weight, ("fsdp", "ctx"), axis=0, tiled=True),
        lax.all_gather(gate_weight, ("fsdp", "ctx"), axis=0, tiled=True),
        lax.all_gather(hidden_weight, ("fsdp", "ctx"), axis=1, tiled=True),
        lax.all_gather(attended_weight, ("fsdp", "ctx"), axis=1, tiled=True),
        lax.all_gather(update_weight, ("fsdp", "ctx"), axis=1, tiled=True),
        lax.all_gather(ffn_up_weight, ("fsdp", "ctx"), axis=0, tiled=True),
        lax.all_gather(ffn_down_weight, ("fsdp", "ctx"), axis=1, tiled=True),
    )


def norm_forward(row_values, gain_vector):
    squares = feature_total(jnp.sum(row_values * row_values, axis=1))
    inverse = lax.rsqrt(squares / D + EPSILON)
    return (row_values * inverse[:, None] * gain_vector[None], inverse)


def norm_backward(row_values, inverse, gain_vector, grad_normed):
    scaled = grad_normed * gain_vector[None]
    inner_sums = feature_total(jnp.sum(scaled * row_values, axis=1))
    grad_rows = (
        inverse[:, None] * scaled
        - row_values * (inverse * inverse * inverse * inner_sums / D)[:, None]
    )
    grad_gain = jnp.sum(grad_normed * row_values * inverse[:, None], axis=0)
    return (grad_rows, grad_gain)


def ema_run(step_keep, log_rate, inputs):
    row_count, ndim, width = inputs.shape
    size = math.gcd(row_count, 128)
    block_count = row_count // size
    flat_rate = log_rate.reshape(ndim * width)
    blocks_in = inputs.reshape(block_count, size, ndim * width)
    keep_blocks = step_keep.reshape(block_count, size)
    index_float = jnp.arange(size).astype(jnp.float32)
    falling = jnp.exp(-index_float[:, None] * flat_rate[None])
    rising = jnp.exp(index_float[:, None] * flat_rate[None])
    carry_scale = rising * jnp.exp(flat_rate)[None]
    lower = index_float[:, None] >= index_float[None, :]

    def one_block(carry, pair):
        block_in, block_keep = pair
        breaks = jnp.cumsum(1.0 - block_keep)
        linked = (lower & (breaks[:, None] == breaks[None, :])).astype(jnp.float32)
        inner = jnp.dot(
            linked,
            block_in * falling,
            precision=lax.Precision.HIGHEST,
            preferred_element_type=jnp.float32,
        )
        chain = (breaks == 0.0).astype(jnp.float32)
        block_states = rising * inner + chain[:, None] * carry_scale * carry[None]
        return (block_states[-1], block_states)

    last_state, all_states = lax.scan(
        one_block, jnp.zeros((ndim * width,), jnp.float32), (blocks_in, keep_blocks)
    )
    return all_states.reshape(row_count, ndim, width)


def prefix_factor(step_keep, log_rate, extra):
    row_count = step_keep.shape[0]
    index_float = jnp.arange(row_count).astype(jnp.float32) + extra
    chain = (jnp.cumsum(1.0 - step_keep) == 0.0).astype(jnp.float32)
    return jnp.exp(index_float[:, None, None] * log_rate[None]) * chain[:, None, None]


def on_device(
    layer_input,
    segment_ids,
    cotangent,
    norm_gain,
    ema_damping,
    ema_eta,
    query_gain,
    key_gain,
    ffn_gain,
    shared_weight,
    value_weight,
    gate_weight,
    hidden_weight,
    attended_weight,
    update_weight,
    ffn_up_weight,
    ffn_down_weight,
):
    tokens = layer_input[0].astype(jnp.float32)
    segment = segment_ids[0]
    row_count = tokens.shape[0]
    local_dim = tokens.shape[1]
    offset = lax.axis_index("ctx") * row_count
    all_ids = lax.all_gather(segment, "ctx", axis=0, tiled=True)
    key_count = all_ids.shape[0]
    earlier_id = lax.dynamic_slice_in_dim(all_ids, jnp.maximum(offset - 1, 0), 1, 0)[0]
    first_keep = jnp.where(
        offset > 0, (segment[0] == earlier_id).astype(jnp.float32), jnp.float32(0.0)
    )
    keep_flags = jnp.concatenate(
        [first_keep[None], (segment[1:] == segment[:-1]).astype(jnp.float32)]
    )
    (
        full_shared,
        full_value,
        full_gate,
        full_hidden,
        full_attended,
        full_update,
        full_up,
        full_down,
    ) = gather_weights(
        shared_weight,
        value_weight,
        gate_weight,
        hidden_weight,
        attended_weight,
        update_weight,
        ffn_up_weight,
        ffn_down_weight,
    )
    normed, inverse_in = norm_forward(tokens, norm_gain)
    log_rate = jnp.log(1.0 - ema_damping)
    local_states = ema_run(keep_flags, log_rate, ema_damping[None] * normed[:, None, :])
    cumulative = prefix_factor(keep_flags, log_rate, 1.0)
    carried = prefix(
        (cumulative[-1], local_states[-1]),
        "ctx",
        linear_pair,
        (jnp.ones_like(cumulative[-1]), jnp.zeros_like(local_states[-1])),
    )
    carry_in = carried[1]
    states = local_states + cumulative * carry_in[None]
    mixed_pre = jnp.sum(ema_eta[None] * states, axis=1) + normed
    mixed_low = jax.nn.silu(mixed_pre).astype(jnp.bfloat16)
    both_full = gather_features(jnp.stack([normed.astype(jnp.bfloat16), mixed_low]))
    normed_full = both_full[0]
    mixed_full = both_full[1]
    shared_pre = multiply(mixed_full, full_shared)
    shared = jax.nn.silu(shared_pre)
    queries = (shared * query_gain[None]).astype(jnp.bfloat16)
    key_rows = (shared * key_gain[None]).astype(jnp.bfloat16)
    value_pre = multiply(normed_full, full_value)
    values = jax.nn.silu(value_pre).astype(jnp.bfloat16)
    gate_pre = multiply(mixed_full, full_gate)
    gate_rows = jax.nn.silu(gate_pre)
    all_keys, all_values = (
        lax.all_gather(key_rows, "ctx", axis=0, tiled=True),
        lax.all_gather(values, "ctx", axis=0, tiled=True),
    )
    block_size = math.gcd(row_count, 512)
    block_count = row_count // block_size
    key_position = jnp.arange(key_count)

    def block_scores(block_index):
        first_row = block_index * block_size
        query_block = lax.dynamic_slice_in_dim(queries, first_row, block_size, 0)
        ids_block = lax.dynamic_slice_in_dim(segment, first_row, block_size, 0)
        query_position = offset + first_row + jnp.arange(block_size)
        raw_scores = multiply_right(query_block, all_keys) / math.sqrt(Z)
        allowed = (query_position[:, None] >= key_position[None, :]) & (
            ids_block[:, None] == all_ids[None, :]
        )
        return (jnp.where(allowed, raw_scores, -1e30), query_block)

    def attend_block(block_index):
        scores, query_block = block_scores(block_index)
        row_peak = jnp.max(scores, axis=1, keepdims=True)
        exponent = jnp.exp(scores - row_peak)
        row_total = jnp.sum(exponent, axis=1, keepdims=True)
        probabilities = (exponent / row_total).astype(jnp.bfloat16)
        return (multiply(probabilities, all_values), (row_peak + jnp.log(row_total))[:, 0])

    attended_blocks, log_blocks = lax.map(attend_block, jnp.arange(block_count))
    attended = attended_blocks.reshape(row_count, -1)
    log_totals = log_blocks.reshape(row_count)
    gated_rows = (gate_rows * attended).astype(jnp.bfloat16)
    partial_value = jnp.stack(
        [
            multiply(mixed_low, full_hidden) + multiply(gated_rows, full_attended),
            multiply(mixed_low, full_update),
        ]
    )
    summed = sum_features(partial_value)
    hidden_pre = summed[0]
    update_pre = summed[1]
    update = jax.nn.sigmoid(update_pre)
    hidden_act = jax.nn.silu(hidden_pre)
    block_out = update * hidden_act + (1.0 - update) * tokens
    ffn_normed, inverse_mid = norm_forward(block_out, ffn_gain)
    ffn_full = gather_features(ffn_normed.astype(jnp.bfloat16)[None])[0]
    up_pre = multiply(ffn_full, full_up)
    up_rows = jax.nn.silu(up_pre).astype(jnp.bfloat16)
    ffn_out = sum_features(multiply(up_rows, full_down)[None])[0]
    result = (block_out + ffn_out).astype(jnp.bfloat16)
    (
        full_shared,
        full_value,
        full_gate,
        full_hidden,
        full_attended,
        full_update,
        full_up,
        full_down,
    ) = gather_weights(
        shared_weight,
        value_weight,
        gate_weight,
        hidden_weight,
        attended_weight,
        update_weight,
        ffn_up_weight,
        ffn_down_weight,
    )
    grad_out = cotangent[0].astype(jnp.float32)
    grad_full = gather_grads(cotangent[0][None])[0]
    grad_down = multiply_left(up_rows, grad_full)
    grad_up_pre = (multiply_right(grad_full, full_down) * silu_grad(up_pre)).astype(jnp.bfloat16)
    grad_up = multiply_left(ffn_full, grad_up_pre)
    grad_ffn_normed = sum_grads(multiply_right(grad_up_pre, full_up)[None])[0]
    grad_mid, grad_ffn_gain = norm_backward(block_out, inverse_mid, ffn_gain, grad_ffn_normed)
    grad_block = grad_out + grad_mid
    grad_update_pre = (grad_block * (hidden_act - tokens) * update * (1.0 - update)).astype(
        jnp.bfloat16
    )
    grad_hidden_pre = (grad_block * update * silu_grad(hidden_pre)).astype(jnp.bfloat16)
    grad_tokens = grad_block * (1.0 - update)
    both_grads = gather_grads(jnp.stack([grad_hidden_pre, grad_update_pre]))
    grad_hidden_full = both_grads[0]
    grad_update_full = both_grads[1]
    grad_hidden_weight = multiply_left(mixed_low, grad_hidden_full)
    grad_update_weight = multiply_left(mixed_low, grad_update_full)
    grad_attended_weight = multiply_left(gated_rows, grad_hidden_full)
    grad_gated = multiply_right(grad_hidden_full, full_attended)
    grad_mixed_local = multiply_right(grad_hidden_full, full_hidden) + multiply_right(
        grad_update_full, full_update
    )
    grad_attended = (grad_gated * gate_rows).astype(jnp.bfloat16)
    grad_gate_pre = (grad_gated * attended * silu_grad(gate_pre)).astype(jnp.bfloat16)

    def backward_block(running, block_index):
        key_sums, value_sums = running
        scores, query_block = block_scores(block_index)
        first_row = block_index * block_size
        exact = jnp.exp(
            scores - lax.dynamic_slice_in_dim(log_totals, first_row, block_size, 0)[:, None]
        )
        grad_block_out = lax.dynamic_slice_in_dim(grad_attended, first_row, block_size, 0)
        value_sums = value_sums + multiply_left(exact.astype(jnp.bfloat16), grad_block_out)
        grad_probs = multiply_right(grad_block_out, all_values)
        row_inner = jnp.sum(exact * grad_probs, axis=1, keepdims=True)
        grad_scores = exact * (grad_probs - row_inner) / math.sqrt(Z)
        scores_high = grad_scores.astype(jnp.bfloat16)
        scores_rest = (grad_scores - scores_high.astype(jnp.float32)).astype(jnp.bfloat16)
        grad_query_block = multiply(scores_high, all_keys) + multiply(scores_rest, all_keys)
        key_sums = (
            key_sums
            + multiply_left(scores_high, query_block)
            + multiply_left(scores_rest, query_block)
        )
        return ((key_sums, value_sums), grad_query_block)

    (key_sums, value_sums), query_blocks = lax.scan(
        backward_block,
        (
            jnp.zeros((key_count, key_rows.shape[1]), jnp.float32),
            jnp.zeros((key_count, values.shape[1]), jnp.float32),
        ),
        jnp.arange(block_count),
    )
    grad_queries = query_blocks.reshape(row_count, -1)
    key_grads, value_grads = (
        lax.psum_scatter(key_sums, "ctx", scatter_dimension=0, tiled=True),
        lax.psum_scatter(value_sums, "ctx", scatter_dimension=0, tiled=True),
    )
    grad_queries, key_grads = lax.psum((grad_queries, key_grads), "tp")
    grad_value_pre = (value_grads * silu_grad(value_pre)).astype(jnp.bfloat16)
    grad_shared = grad_queries * query_gain[None] + key_grads * key_gain[None]
    grad_query_gain = jnp.sum(shared * grad_queries, axis=0)
    grad_key_gain = jnp.sum(shared * key_grads, axis=0)
    grad_shared_pre = (grad_shared * silu_grad(shared_pre)).astype(jnp.bfloat16)
    grad_shared_weight = multiply_left(mixed_full, grad_shared_pre)
    grad_value_weight = multiply_left(normed_full, grad_value_pre)
    grad_gate_weight = multiply_left(mixed_full, grad_gate_pre)
    own_shared = lax.dynamic_slice_in_dim(
        full_shared, lax.axis_index("tp") * local_dim, local_dim, 0
    )
    grad_mixed_local = grad_mixed_local + multiply_right(grad_shared_pre, own_shared)
    back_sums = sum_grads(
        jnp.stack(
            [multiply_right(grad_value_pre, full_value), multiply_right(grad_gate_pre, full_gate)]
        )
    )
    grad_mix_pre = (grad_mixed_local + back_sums[1]) * silu_grad(mixed_pre)
    grad_eta = jnp.sum(states * grad_mix_pre[:, None, :], axis=0)
    grad_states = ema_eta[None] * grad_mix_pre[:, None, :]
    keep_next = jnp.concatenate([keep_flags[1:], jnp.ones((1,), jnp.float32)])
    reversed_keep = keep_next[::-1]
    adjoint_local = ema_run(reversed_keep, log_rate, grad_states[::-1])[::-1]
    reverse_products = prefix_factor(reversed_keep, log_rate, 0.0)[::-1]
    first_adjoint = keep_flags[0] * (1.0 - ema_damping) * adjoint_local[0]
    from_later = entering(
        (cumulative[-1], first_adjoint),
        "ctx",
        linear_pair,
        (jnp.ones_like(first_adjoint), jnp.zeros_like(first_adjoint)),
    )
    adjoint = adjoint_local + reverse_products * from_later[1][None]
    previous = jnp.concatenate([carry_in[None], states[:-1]], axis=0)
    grad_damping = jnp.sum(
        adjoint * (normed[:, None, :] - keep_flags[:, None, None] * previous), axis=0
    )
    grad_normed = back_sums[0] + grad_mix_pre + jnp.sum(ema_damping[None] * adjoint, axis=1)
    grad_in, grad_norm_gain = norm_backward(tokens, inverse_in, norm_gain, grad_normed)
    grad_tokens = grad_tokens + grad_in
    small_sums = lax.psum(
        (grad_norm_gain, grad_damping, grad_eta, grad_query_gain, grad_key_gain, grad_ffn_gain),
        ("fsdp", "ctx"),
    )
    weight_sums = (
        lax.psum_scatter(grad_shared_weight, ("fsdp", "ctx"), scatter_dimension=0, tiled=True),
        lax.psum_scatter(grad_value_weight, ("fsdp", "ctx"), scatter_dimension=0, tiled=True),
        lax.psum_scatter(grad_gate_weight, ("fsdp", "ctx"), scatter_dimension=0, tiled=True),
        lax.psum_scatter(grad_hidden_weight, ("fsdp", "ctx"), scatter_dimension=1, tiled=True),
        lax.psum_scatter(grad_attended_weight, ("fsdp", "ctx"), scatter_dimension=1, tiled=True),
        lax.psum_scatter(grad_update_weight, ("fsdp", "ctx"), scatter_dimension=1, tiled=True),
        lax.psum_scatter(grad_up, ("fsdp", "ctx"), scatter_dimension=0, tiled=True),
        lax.psum_scatter(grad_down, ("fsdp", "ctx"), scatter_dimension=1, tiled=True),
    )
    return (
        result[None],
        grad_tokens[None],
        small_sums[0],
        small_sums[1],
        small_sums[2],
        small_sums[3],
        small_sums[4],
        small_sums[5],
        weight_sums[0],
        weight_sums[1],
        weight_sums[2],
        weight_sums[3],
        weight_sums[4],
        weight_sums[5],
        weight_sums[6],
        weight_sums[7],
    )


def solution(mesh):
    placed = (
        P("fsdp", "ctx", "tp"),
        P("fsdp", "ctx"),
        P("fsdp", "ctx", "tp"),
        P("tp"),
        P(None, "tp"),
        P(None, "tp"),
        P(),
        P(),
        P("tp"),
        P(("fsdp", "ctx"), None),
        P(("fsdp", "ctx"), "tp"),
        P(("fsdp", "ctx"), "tp"),
        P("tp", ("fsdp", "ctx")),
        P("tp", ("fsdp", "ctx")),
        P("tp", ("fsdp", "ctx")),
        P(("fsdp", "ctx"), "tp"),
        P("tp", ("fsdp", "ctx")),
    )
    return jax.shard_map(
        on_device,
        mesh=mesh,
        in_specs=placed,
        out_specs=(
            P("fsdp", "ctx", "tp"),
            P("fsdp", "ctx", "tp"),
            P("tp"),
            P(None, "tp"),
            P(None, "tp"),
            P(),
            P(),
            P("tp"),
            P(("fsdp", "ctx"), None),
            P(("fsdp", "ctx"), "tp"),
            P(("fsdp", "ctx"), "tp"),
            P("tp", ("fsdp", "ctx")),
            P("tp", ("fsdp", "ctx")),
            P("tp", ("fsdp", "ctx")),
            P(("fsdp", "ctx"), "tp"),
            P("tp", ("fsdp", "ctx")),
        ),
        check_vma=False,
    )
```

profile of v0, /device:TPU:0, one launch (start us, length us, event | category | flops | bytes accessed | tf_op | source)
XLA Modules:
  0.0 1236.1 jit_solution(14677768598098796378)
XLA Ops:
  14.7 11.2 psum.84
  32.6 7.2 mul.628
  39.8 18.2 %mul.629 = f32[8,128,4096]{2,1,0:T(8,128)} reshape(f32[1024,16,256]{2,1,0:T(8,128)} %mul.628) | data formatting | bytes 33554432 | tf_op jit(solution)/shard_map/mul | solution.py:233
  57.9 12.3 broadcast_multiply_fusion.1
  70.2 8.0 broadcast.270.clone
  78.2 44.5 %while.88 = (s32[]{:T(128)}, f32[4096]{0:T(1024)S(1)}, f32[8,128,4096]{2,1,0:T(8,128)}, f32[8,128]{1,0:T(8,128)S(1)}, f32[8,128,4096]{2,1,0:T(8,128)}, /*index=5...) while((s32[]{:T(128)}, f32[4096]{0:T(1024)S(1)}, ...), condition=%wide.region_4.5_spmd.clone.clone, body=%wide.region_2.4_spmd.clone.clone.sunk | while | flops 809566464 | bytes 6399625 | solution.py:166
  78.6 5.1 bitcast_dynamic-update-slice_fusion.4
  84.2 5.1 bitcast_dynamic-update-slice_fusion.4
  89.8 5.1 bitcast_dynamic-update-slice_fusion.4
  95.3 5.1 bitcast_dynamic-update-slice_fusion.4
  106.4 5.2 bitcast_dynamic-update-slice_fusion.4
  117.6 5.1 bitcast_dynamic-update-slice_fusion.4
  122.7 11.0 copy.41
  135.6 8.9 exponential_multiply_fusion
  144.5 5.8 copy-done.8
  152.4 16.9 %multiply_reduce_fusion.3 = (f32[1024,256]{1,0:T(8,128)S(1)}, f32[1024,16,256]{2,1,0:T(8,128)}) fusion(f32[16,256]{1,0:T(8,128)S(1)} %copy-done.44, f32[16,256]{1,0:T(8,128)S(1)} %get-tuple-element.421, f32[1024]{0:T(1024)S(1)} %fusion.199, f32[16,256]{1,0:T(8,128)S(1)} %get-tuple-element.790, f32[1024]{0:T(1024)S(1)} %broadcast_add_fusion, ...), kind=kLoop, calls=%fused_computation.106 | loop fusion | flops 24903680 | bytes 34660352 | tf_op jit(solution)/shard_map/reduce_sum | solution.py:243
  171.7 52.0 %all-gather.13.cloned.1.call-done = bf16[2,1024,1024]{2,1,0:T(8,128)(2,1)} async-done(((bf16[2,1024,256]{2,1,0:T(8,128)(2,1)}), bf16[2,1024,1024]{2,1,0:T(8,128)(2,1)}) %all-gather.13.cloned.1.call-update) | async-done | bytes 4194320 | tf_op jit(solution)/shard_map/all_gather | solution.py:85
  229.9 14.2 %all_gather.75 = bf16[1024,128]{1,0:T(8,128)(2,1)S(1)} all-gather(bf16[128,128]{1,0:T(8,128)(2,1)S(1)} %copy-done.54), channel_id=1, replica_groups=mesh['fsdp'=4,'ctx'=2,'tp'=4] {'fsdp','ctx'}, dimensions={0}, use_global_device_ids=true | all-gather | bytes 294912 | tf_op jit(solution)/shard_map/all_gather | solution.py:111
  244.2 15.3 %all_gather.72 = bf16[256,1024]{1,0:T(8,128)(2,1)S(1)} all-gather(bf16[256,128]{1,0:T(8,128)(2,1)S(1)} %copy-done.46), channel_id=1, replica_groups=mesh['fsdp'=4,'ctx'=2,'tp'=4] {'fsdp','ctx'}, dimensions={1}, use_global_device_ids=true | all-gather | bytes 589824 | tf_op jit(solution)/shard_map/all_gather | solution.py:114
  259.5 14.1 %all_gather.80 = bf16[256,1024]{1,0:T(8,128)(2,1)S(1)} all-gather(bf16[256,128]{1,0:T(8,128)(2,1)S(1)} %copy-done.47), channel_id=1, replica_groups=mesh['fsdp'=4,'ctx'=2,'tp'=4] {'fsdp','ctx'}, dimensions={1}, use_global_device_ids=true | all-gather | bytes 589824 | tf_op jit(solution)/shard_map/all_gather | solution.py:116
  283.6 12.6 %while.85 = (s32[]{:T(128)}, f32[2,512,512]{2,1,0:T(8,128)}, f32[2,512]{1,0:T(2,128)S(1)}, s32[2]{0:T(128)S(1)}, s32[]{:T(128)}, /*index=5*/s32[1024]{0:T(1024)S...) while((s32[]{:T(128)}, f32[2,512,512]{2,1,0:T(8,128)}, ...), condition=%wide.region_13.14_spmd.clone, body=%wide.region_10.13_spmd.clone.sunk | while | flops 1353711616 | bytes 41589048 | solution.py:283
  296.2 5.3 fusion.86
  310.7 85.5 %reduce-scatter.15.cloned.1.call-done = f32[2,1024,256]{2,1,0:T(8,128)} async-done(((f32[2,1024,1024]{2,1,0:T(8,128)}), f32[2,1024,256]{2,1,0:T(8,128)}) %reduce-scatter.15.cloned.1.call-update) | async-done | bytes 2097168 | tf_op jit(solution)/shard_map/reduce_scatter | solution.py:89
  399.4 8.9 psum.85
  411.9 15.0 %all-gather.25.cloned.1.call-done = bf16[1024,1024]{1,0:T(8,128)(2,1)} async-done(((bf16[128,1024]{1,0:T(8,128)(2,1)}), bf16[1024,1024]{1,0:T(8,128)(2,1)}) %all-gather.25.cloned.1.call-update) | async-done | bytes 2097168 | tf_op jit(solution)/shard_map/all_gather | solution.py:117
  427.0 37.2 %all-gather.23.cloned.1.call-done = bf16[1,1024,1024]{2,1,0:T(8,128)(2,1)} async-done(((bf16[1,1024,256]{2,1,0:T(8,128)(2,1)}), bf16[1,1024,1024]{2,1,0:T(8,128)(2,1)}) %all-gather.23.cloned.1.call-update) | async-done | bytes 2097168 | tf_op jit(solution)/shard_map/all_gather | solution.py:85
  464.2 6.6 fusion.84
  470.8 30.6 %all-gather.29.cloned.1.call-done = bf16[1,1024,1024]{2,1,0:T(8,128)(2,1)} async-done(((bf16[1,1024,256]{2,1,0:T(8,128)(2,1)}), bf16[1,1024,1024]{2,1,0:T(8,128)(2,1)}) %all-gather.29.cloned.1.call-update) | async-done | bytes 2097168 | tf_op jit(solution)/shard_map/all_gather | solution.py:93
  501.4 32.4 %all-gather.27.cloned.1.call-done = bf16[1024,1024]{1,0:T(8,128)(2,1)} async-done(((bf16[1024,128]{1,0:T(8,128)(2,1)}), bf16[1024,1024]{1,0:T(8,128)(2,1)}) %all-gather.27.cloned.1.call-update) | async-done | bytes 2097168 | tf_op jit(solution)/shard_map/all_gather | solution.py:118
  533.8 6.7 multiply_convert_fusion
  546.2 7.3 convolution_bitcast_fusion.3
  553.6 44.5 %reduce-scatter.19.cloned.1.call-done = f32[1,1024,256]{2,1,0:T(8,128)} async-done(((f32[1,1024,1024]{2,1,0:T(8,128)}), f32[1,1024,256]{2,1,0:T(8,128)}) %reduce-scatter.19.cloned.1.call-update) | async-done | bytes 1048592 | tf_op jit(solution)/shard_map/reduce_scatter | solution.py:97
  600.5 8.9 psum.86
  609.5 44.1 %reduce-scatter.17.cloned.1.call-done = f32[1,1024,256]{2,1,0:T(8,128)} async-done(((f32[1,1024,1024]{2,1,0:T(8,128)}), f32[1,1024,256]{2,1,0:T(8,128)}) %reduce-scatter.17.cloned.1.call-update) | async-done | bytes 1048592 | tf_op jit(solution)/shard_map/reduce_scatter | solution.py:89
  658.3 52.4 %all-gather.31.cloned.1.call-done = bf16[2,1024,1024]{2,1,0:T(8,128)(2,1)} async-done(((bf16[2,1024,256]{2,1,0:T(8,128)(2,1)}), bf16[2,1024,1024]{2,1,0:T(8,128)(2,1)}) %all-gather.31.cloned.1.call-update) | async-done | bytes 4194320 | tf_op jit(solution)/shard_map/all_gather | solution.py:93
  710.7 6.2 fusion.88
  716.9 26.3 %while.87 = (s32[]{:T(128)}, f32[2048,128]{1,0:T(8,128)S(1)}, f32[2048,512]{1,0:T(8,128)}, f32[2,512,128]{2,1,0:T(8,128)S(1)}, s32[2]{0:T(128)S(1)}, /*index=5*/...) while((s32[]{:T(128)}, f32[2048,128]{1,0:T(8,128)S(1)}, ...), condition=%wide.region_23.24_spmd.clone, body=%wide.region_21.23_spmd.clone.sunk | while | flops 3509387264 | bytes 89813328 | solution.py:372
  753.4 14.9 %reduce-scatter.21.cloned.1.call-done = f32[1024,512]{1,0:T(8,128)} async-done(((f32[2048,512]{1,0:T(8,128)}), f32[1024,512]{1,0:T(8,128)}) %reduce-scatter.21.cloned.1.call-update) | async-done | bytes 2097168 | tf_op jit(solution)/shard_map/reduce_scatter | solution.py:383
  779.2 6.6 fusion.79
  787.4 6.0 fusion.82
  810.1 15.4 %all-reduce.4.cloned.1.call-done = (f32[1024,128]{1,0:T(8,128)}, f32[1024,128]{1,0:T(8,128)}) async-done(((f32[1024,128]{1,0:T(8,128)}, f32[1024,128]{1,0:T(8,128)}), (f32[1024,128]{1,0:T(8,128)}, f32[1024,128]{1,0:T(8,128)})) %all-reduce.4.cloned.1.call-update) | async-done | bytes 1048592 | tf_op jit(solution)/shard_map/psum | solution.py:385
  831.0 12.1 slice.108
  853.9 61.2 %reduce-scatter.23.cloned.1.call-done = f32[2,1024,256]{2,1,0:T(8,128)} async-done(((f32[2,1024,1024]{2,1,0:T(8,128)}), f32[2,1024,256]{2,1,0:T(8,128)}) %reduce-scatter.23.cloned.1.call-update) | async-done | bytes 2097168 | tf_op jit(solution)/shard_map/reduce_scatter | solution.py:97
  917.4 8.2 broadcast_multiply_fusion
  925.5 11.9 rev.13
  937.4 18.3 %reshape.409 = f32[8,128,4096]{2,1,0:T(8,128)} reshape(f32[1024,16,256]{2,1,0:T(8,128)} %rev.13) | data formatting | bytes 33554432 | tf_op jit(solution)/shard_map/reshape | solution.py:144
  955.7 7.9 broadcast.270
  963.6 49.8 %while.89 = (s32[]{:T(128)}, f32[4096]{0:T(1024)S(1)}, f32[8,128,4096]{2,1,0:T(8,128)}, f32[8,128]{1,0:T(8,128)}, f32[8,128,4096]{2,1,0:T(8,128)}, /*index=5*/f3...) while((s32[]{:T(128)}, f32[4096]{0:T(1024)S(1)}, ...), condition=%wide.region_31.32_spmd.clone.clone, body=%wide.region_29.31_spmd.clone.clone.sunk | while | flops 809566464 | bytes 6399625 | solution.py:166
  970.9 5.1 bitcast_dynamic-update-slice_fusion.5
  983.3 5.1 bitcast_dynamic-update-slice_fusion.5
  989.6 5.1 bitcast_dynamic-update-slice_fusion.5
  995.8 5.2 bitcast_dynamic-update-slice_fusion.5
  1002.1 5.1 bitcast_dynamic-update-slice_fusion.5
  1008.3 5.1 bitcast_dynamic-update-slice_fusion.5
  1013.4 7.1 mul.716
  1020.6 18.2 %mul.749 = f32[8,128,4096]{2,1,0:T(8,128)} reshape(f32[1024,16,256]{2,1,0:T(8,128)} %mul.716) | data formatting | bytes 33554432 | tf_op jit(solution)/shard_map/mul | solution.py:405
  1038.8 13.4 %multiply_reduce_fusion.1 = f32[4096]{0:T(1024)S(1)} fusion(f32[8,128,4096]{2,1,0:T(8,128)} %mul.749, f32[8,128,4096]{2,1,0:T(8,128)} %get-tuple-element.420, f32[4096]{0:T(1024)S(1)} %bitcast.355, f32[8,128]{1,0:T(8,128)S(1)} %fusion.152, f32[4096]{0:T(1024)S(1)} %get-tuple-element.1428, f32[8,128]{1,0:T(8,128)S(1)} %convert_add_fusion.1), kind=kLoop, calls=%fused_computation.102 | loop fusion | flops 25161728 | bytes 33611776 | tf_op jit(solution)/shard_map/reduce_sum | solution.py:404
  1054.5 10.2 copy.43
  1067.3 18.0 %fusion.78 = (f32[16,256]{1,0:T(8,128)S(1)}, f32[1024,256]{1,0:T(8,128)S(1)}) fusion(f32[1023,16,256]{2,1,0:T(8,128)} %slice.108, f32[1,16,256]{2,1,0:T(8,128)S(1)} %bitcast.347, f32[1024]{0:T(1024)S(1)} %bitcast.361, f32[1024,256]{1,0:T(8,128)S(1)} %copy-done.11, f32[16,256]{1,0:T(8,128)S(1)} %get-tuple-element.428, ...), kind=kLoop, calls=%fused_computation.101 | loop fusion | flops 37482496 | bytes 52482048 | tf_op jit(solution)/shard_map/reduce_sum | solution.py:419
  1086.8 30.4 %all-reduce = (f32[256]{0:T(256)}, f32[16,256]{1,0:T(8,128)}, f32[16,256]{1,0:T(8,128)}, f32[128]{0:T(128)}, f32[128]{0:T(128)}, /*index=5*/f32[256]{0:T(256)}) all-reduce(f32[256]{0:T(256)S(1)} %get-tuple-element.645, f32[16,256]{1,0:T(8,128)S(1)} %get-tuple-element.641, ...), channel_id=1, replica_groups=mesh['fsdp'=4,'ctx'=2,'tp'=4] {'fsdp','ctx'}, use_global_device_ids=true, to_apply=%region_40.41 | all-reduce | flops 8960 | bytes 71680 | tf_op jit(solution)/shard_map/psum | solution.py:425
  1117.2 8.9 psum.89
  1129.3 30.9 %reduce-scatter.31.cloned.1.call-done = f32[128,512]{1,0:T(8,128)} async-done(((f32[1024,512]{1,0:T(8,128)}), f32[128,512]{1,0:T(8,128)}) %reduce-scatter.31.cloned.1.call-update) | async-done | bytes 262160 | tf_op jit(solution)/shard_map/reduce_scatter | solution.py:432
  1160.2 32.1 %reduce-scatter.27.cloned.1.call-done = f32[128,128]{1,0:T(8,128)} async-done(((f32[1024,128]{1,0:T(8,128)}), f32[128,128]{1,0:T(8,128)}) %reduce-scatter.27.cloned.1.call-update) | async-done | bytes 65552 | tf_op jit(solution)/shard_map/reduce_scatter | solution.py:430
  1192.4 37.0 %reduce-scatter.29.cloned.1.call-done = f32[128,512]{1,0:T(8,128)} async-done(((f32[1024,512]{1,0:T(8,128)}), f32[128,512]{1,0:T(8,128)}) %reduce-scatter.29.cloned.1.call-update) | async-done | bytes 262160 | tf_op jit(solution)/shard_map/reduce_scatter | solution.py:431
  (480 shorter events, 200.1 us)
Async XLA Ops:
  7.2 164.6 %all-gather.17.cloned.1.call-start = ((), (), s32[]{:S(2)}) async-start(), calls=%async_computation.16 | async-start | bytes 1179648 | tf_op jit(solution)/shard_map/all_gather | solution.py:112
  7.9 215.8 %all-gather.13.cloned.1.call-start = ((), (), s32[]{:S(2)}) async-start(), calls=%async_computation.14 | async-start | bytes 5242880 | tf_op jit(solution)/shard_map/all_gather | solution.py:85
  25.9 250.5 %copy-start.42 = (f32[1024]{0:T(1024)}, f32[1024]{0:T(1024)S(1)}, u32[]{:S(2)}) copy-start(f32[1024]{0:T(1024)S(1)} %add_rsqrt_fusion.1) | copy-start | bytes 12292
  135.6 16.8 %copy-start.44 = (f32[16,256]{1,0:T(8,128)S(1)}, f32[16,256]{1,0:T(8,128)}, u32[]{:S(2)}) copy-start(f32[16,256]{1,0:T(8,128)} %param.34) | copy-start | bytes 49156
  152.4 16.9 %copy-start.26 = (f32[16,256]{1,0:T(8,128)}, f32[16,256]{1,0:T(8,128)S(1)}, u32[]{:S(2)}) copy-start(f32[16,256]{1,0:T(8,128)S(1)} %get-tuple-element.421) | copy-start | bytes 49156
  152.4 16.9 %copy-start.4 = (bf16[1,1024,256]{2,1,0:T(8,128)(2,1)S(1)}, bf16[1,1024,256]{2,1,0:T(8,128)(2,1)}, u32[]{:S(2)}) copy-start(bf16[1,1024,256]{2,1,0:T(8,128)(2,1)} %param.29) | copy-start | bytes 1572868
  152.4 16.9 %copy-start.60 = (f32[256]{0:T(256)S(1)}, f32[256]{0:T(256)}, u32[]{:S(2)}) copy-start(f32[256]{0:T(256)} %param.32) | copy-start | bytes 3076
  169.3 107.1 %copy-start.19 = (f32[1024,256]{1,0:T(8,128)}, f32[1024,256]{1,0:T(8,128)S(1)}, u32[]{:S(2)}) copy-start(f32[1024,256]{1,0:T(8,128)S(1)} %get-tuple-element.766) | copy-start | bytes 3145732
  171.6 58.3 %copy-start.54 = (bf16[128,128]{1,0:T(8,128)(2,1)S(1)}, bf16[128,128]{1,0:T(8,128)(2,1)}, u32[]{:S(2)}) copy-start(bf16[128,128]{1,0:T(8,128)(2,1)} %param.38) | copy-start | bytes 98308
  171.6 72.6 %copy-start.46 = (bf16[256,128]{1,0:T(8,128)(2,1)S(1)}, bf16[256,128]{1,0:T(8,128)(2,1)}, u32[]{:S(2)}) copy-start(bf16[256,128]{1,0:T(8,128)(2,1)} %param.41) | copy-start | bytes 196612
  171.7 87.8 %copy-start.47 = (bf16[256,128]{1,0:T(8,128)(2,1)S(1)}, bf16[256,128]{1,0:T(8,128)(2,1)}, u32[]{:S(2)}) copy-start(bf16[256,128]{1,0:T(8,128)(2,1)} %param.43) | copy-start | bytes 196612
  171.7 111.9 %all-gather.19.cloned.1.call-start = ((), (), s32[]{:S(2)}) async-start(), calls=%async_computation.17 | async-start | bytes 3145728 | tf_op jit(solution)/shard_map/all_gather | solution.py:258
  228.7 67.5 %all-gather.15.cloned.1.call-start = ((), (), s32[]{:S(2)}) async-start(), calls=%async_computation.15 | async-start | bytes 1179648 | tf_op jit(solution)/shard_map/all_gather | solution.py:113
  229.3 72.2 %all-gather.21.cloned.1.call-start = ((), (), s32[]{:S(2)}) async-start(), calls=%async_computation.18 | async-start | bytes 1179648 | tf_op jit(solution)/shard_map/all_gather | solution.py:115
  229.9 166.3 %reduce-scatter.15.cloned.1.call-start = ((), (), s32[]{:S(2)}) async-start(), calls=%async_computation.19 | async-start | bytes 10485760 | tf_op jit(solution)/shard_map/reduce_scatter | solution.py:89
  244.2 35.1 %copy-start.36 = (bf16[1024,128]{1,0:T(8,128)(2,1)}, bf16[1024,128]{1,0:T(8,128)(2,1)S(1)}, u32[]{:S(2)}) copy-start(bf16[1024,128]{1,0:T(8,128)(2,1)S(1)} %all_gather.75) | copy-start | bytes 786436
  259.5 19.8 %copy-start.30 = (bf16[256,1024]{1,0:T(8,128)(2,1)}, bf16[256,1024]{1,0:T(8,128)(2,1)S(1)}, u32[]{:S(2)}) copy-start(bf16[256,1024]{1,0:T(8,128)(2,1)S(1)} %all_gather.72) | copy-start | bytes 1572868
  309.8 98.5 %copy-start.62 = (f32[256]{0:T(256)S(1)}, f32[256]{0:T(256)}, u32[]{:S(2)}) copy-start(f32[256]{0:T(256)} %param.37) | copy-start | bytes 3076
  309.9 117.1 %all-gather.25.cloned.1.call-start = ((), (), s32[]{:S(2)}) async-start(), calls=%async_computation.21 | async-start | bytes 2359296 | tf_op jit(solution)/shard_map/all_gather | solution.py:117
  310.6 153.6 %all-gather.23.cloned.1.call-start = ((), (), s32[]{:S(2)}) async-start(), calls=%async_computation.20 | async-start | bytes 2621440 | tf_op jit(solution)/shard_map/all_gather | solution.py:85
  408.3 245.3 %copy-start.40 = (f32[1024]{0:T(1024)}, f32[1024]{0:T(1024)S(1)}, u32[]{:S(2)}) copy-start(f32[1024]{0:T(1024)S(1)} %add_rsqrt_fusion) | copy-start | bytes 12292
  410.1 91.3 %all-gather.29.cloned.1.call-start = ((), (), s32[]{:S(2)}) async-start(), calls=%async_computation.24 | async-start | bytes 2621440 | tf_op jit(solution)/shard_map/all_gather | solution.py:93
  410.8 122.9 %all-gather.27.cloned.1.call-start = ((), (), s32[]{:S(2)}) async-start(), calls=%async_computation.22 | async-start | bytes 2359296 | tf_op jit(solution)/shard_map/all_gather | solution.py:118
  411.4 186.6 %reduce-scatter.19.cloned.1.call-start = ((), (), s32[]{:S(2)}) async-start(), calls=%async_computation.25 | async-start | bytes 5242880 | tf_op jit(solution)/shard_map/reduce_scatter | solution.py:97
  546.2 107.4 %reduce-scatter.17.cloned.1.call-start = ((), (), s32[]{:S(2)}) async-start(), calls=%async_computation.23 | async-start | bytes 5242880 | tf_op jit(solution)/shard_map/reduce_scatter | solution.py:89
  553.5 157.2 %all-gather.31.cloned.1.call-start = ((), (), s32[]{:S(2)}) async-start(), calls=%async_computation.26 | async-start | bytes 5242880 | tf_op jit(solution)/shard_map/all_gather | solution.py:93
  609.5 48.6 %copy-start.50 = (f32[1024]{0:T(1024)}, f32[1024]{0:T(1024)S(1)}, u32[]{:S(2)}) copy-start(f32[1024]{0:T(1024)S(1)} %fusion.149) | copy-start | bytes 12292
  658.0 94.9 %reduce-scatter.25.cloned.1.call-start = ((), (), s32[]{:S(2)}) async-start(), calls=%async_computation.29 | async-start | bytes 1572864 | tf_op jit(solution)/shard_map/reduce_scatter | solution.py:382
  744.2 24.1 %reduce-scatter.21.cloned.1.call-start = ((), (), s32[]{:S(2)}) async-start(), calls=%async_computation.27 | async-start | bytes 6291456 | tf_op jit(solution)/shard_map/reduce_scatter | solution.py:383
  744.8 80.7 %all-reduce.4.cloned.1.call-start = ((), (), s32[]{:S(2)}) async-start(), calls=%async_computation.38 | async-start | bytes 2097152 | tf_op jit(solution)/shard_map/psum | solution.py:385
  744.8 23.4 %copy-start.25 = (f32[1024,512]{1,0:T(8,128)S(1)}, f32[1024,512]{1,0:T(8,128)}, u32[]{:S(2)}) copy-start(f32[1024,512]{1,0:T(8,128)} %get-tuple-element.794) | copy-start | bytes 6291460
  752.9 17.7 %copy-start.76 = (bf16[1024,512]{1,0:T(8,128)(2,1)S(1)}, bf16[1024,512]{1,0:T(8,128)(2,1)}, u32[]{:S(2)}) copy-start(bf16[1024,512]{1,0:T(8,128)(2,1)} %all-gather.17.cloned.1.call-done) | copy-start | bytes 3145732
  752.9 162.2 %reduce-scatter.23.cloned.1.call-start = ((), (), s32[]{:S(2)}) async-start(), calls=%async_computation.28 | async-start | bytes 10485760 | tf_op jit(solution)/shard_map/reduce_scatter | solution.py:97
  777.3 352.0 %reduce-scatter.41.cloned.1.call-start = ((), (), s32[]{:S(2)}) async-start(), calls=%async_computation.37 | async-start | bytes 4718592 | tf_op jit(solution)/shard_map/reduce_scatter | solution.py:437
  785.8 343.4 %reduce-scatter.39.cloned.1.call-start = ((), (), s32[]{:S(2)}) async-start(), calls=%async_computation.36 | async-start | bytes 4718592 | tf_op jit(solution)/shard_map/reduce_scatter | solution.py:436
  793.4 335.8 %reduce-scatter.33.cloned.1.call-start = ((), (), s32[]{:S(2)}) async-start(), calls=%async_computation.33 | async-start | bytes 1179648 | tf_op jit(solution)/shard_map/reduce_scatter | solution.py:433
  797.8 331.5 %reduce-scatter.37.cloned.1.call-start = ((), (), s32[]{:S(2)}) async-start(), calls=%async_computation.35 | async-start | bytes 1179648 | tf_op jit(solution)/shard_map/reduce_scatter | solution.py:435
  801.2 328.1 %reduce-scatter.35.cloned.1.call-start = ((), (), s32[]{:S(2)}) async-start(), calls=%async_computation.34 | async-start | bytes 2359296 | tf_op jit(solution)/shard_map/reduce_scatter | solution.py:434
  805.6 19.9 %copy-start.34 = (f32[1024,128]{1,0:T(8,128)S(1)}, f32[1024,128]{1,0:T(8,128)}, u32[]{:S(2)}) copy-start(f32[1024,128]{1,0:T(8,128)} %get-tuple-element.792) | copy-start | bytes 1572868
  805.6 19.9 %copy-start.68 = (f32[128]{0:T(128)S(1)}, f32[128]{0:T(128)}, u32[]{:S(2)}) copy-start(f32[128]{0:T(128)} %param.36) | copy-start | bytes 1540
  805.6 19.9 %copy-start.70 = (f32[128]{0:T(128)S(1)}, f32[128]{0:T(128)}, u32[]{:S(2)}) copy-start(f32[128]{0:T(128)} %param.35) | copy-start | bytes 1540
  805.6 354.6 %reduce-scatter.31.cloned.1.call-start = ((), (), s32[]{:S(2)}) async-start(), calls=%async_computation.32 | async-start | bytes 2359296 | tf_op jit(solution)/shard_map/reduce_scatter | solution.py:432
  810.0 21.0 %copy-start.27 = (f32[16,256]{1,0:T(8,128)S(1)}, f32[16,256]{1,0:T(8,128)}, u32[]{:S(2)}) copy-start(f32[16,256]{1,0:T(8,128)} %copy-done.26) | copy-start | bytes 49156
  810.0 382.4 %reduce-scatter.27.cloned.1.call-start = ((), (), s32[]{:S(2)}) async-start(), calls=%async_computation.30 | async-start | bytes 589824 | tf_op jit(solution)/shard_map/reduce_scatter | solution.py:430
  830.2 399.1 %reduce-scatter.29.cloned.1.call-start = ((), (), s32[]{:S(2)}) async-start(), calls=%async_computation.31 | async-start | bytes 2359296 | tf_op jit(solution)/shard_map/reduce_scatter | solution.py:431
  831.0 14.1 %copy-start.31 = (bf16[256,1024]{1,0:T(8,128)(2,1)S(1)}, bf16[256,1024]{1,0:T(8,128)(2,1)}, u32[]{:S(2)}) copy-start(bf16[256,1024]{1,0:T(8,128)(2,1)} %copy-done.30) | copy-start | bytes 1572868
  831.0 16.5 %copy-start.24 = (bf16[256,1024]{1,0:T(8,128)(2,1)S(1)}, bf16[256,1024]{1,0:T(8,128)(2,1)}, u32[]{:S(2)}) copy-start(bf16[256,1024]{1,0:T(8,128)(2,1)} %copy-done.23) | copy-start | bytes 1572868
  849.3 65.8 %copy-start.5 = (bf16[1,1024,256]{2,1,0:T(8,128)(2,1)S(1)}, bf16[1,1024,256]{2,1,0:T(8,128)(2,1)}, u32[]{:S(2)}) copy-start(bf16[1,1024,256]{2,1,0:T(8,128)(2,1)} %param.29) | copy-start | bytes 1572868
  849.3 65.8 %copy-start.20 = (f32[1024,256]{1,0:T(8,128)S(1)}, f32[1024,256]{1,0:T(8,128)}, u32[]{:S(2)}) copy-start(f32[1024,256]{1,0:T(8,128)} %copy-done.19) | copy-start | bytes 3145732
  849.3 65.8 %copy-start.43 = (f32[1024]{0:T(1024)S(1)}, f32[1024]{0:T(1024)}, u32[]{:S(2)}) copy-start(f32[1024]{0:T(1024)} %copy-done.42) | copy-start | bytes 12292
  849.3 65.8 %copy-start.61 = (f32[256]{0:T(256)S(1)}, f32[256]{0:T(256)}, u32[]{:S(2)}) copy-start(f32[256]{0:T(256)} %param.32) | copy-start | bytes 3076
  853.9 63.5 %copy-start.45 = (f32[16,256]{1,0:T(8,128)S(1)}, f32[16,256]{1,0:T(8,128)}, u32[]{:S(2)}) copy-start(f32[16,256]{1,0:T(8,128)} %param.34) | copy-start | bytes 49156
  917.4 96.1 %copy-start.12 = (f32[1024,256]{1,0:T(8,128)}, f32[1024,256]{1,0:T(8,128)S(1)}, u32[]{:S(2)}) copy-start(f32[1024,256]{1,0:T(8,128)S(1)} %fusion.101) | copy-start | bytes 3145732
  1038.8 13.4 %slice-start.1 = ((s8[16777216]{0:T(1024)(128)(4,1)}), s8[4194304]{0:T(1024)(128)(4,1)S(1)}, s32[]{:S(2)}) async-start(s8[16777216]{0:T(1024)(128)(4,1)} %bitcast.343), calls=%async_computation.40 | async-start | bytes 8388608
  1038.8 14.5 %slice-start.2 = ((s8[16777216]{0:T(1024)(128)(4,1)}), s8[4194304]{0:T(1024)(128)(4,1)S(1)}, s32[]{:S(2)}) async-start(s8[16777216]{0:T(1024)(128)(4,1)} %bitcast.343), calls=%async_computation.41 | async-start | bytes 8388608
  1038.8 15.7 %slice-start.3 = ((s8[16777216]{0:T(1024)(128)(4,1)}), s8[4194304]{0:T(1024)(128)(4,1)S(1)}, s32[]{:S(2)}) async-start(s8[16777216]{0:T(1024)(128)(4,1)} %bitcast.343), calls=%async_computation.42 | async-start | bytes 8388608
  1067.3 18.1 %copy-start.13 = (f32[1024,256]{1,0:T(8,128)S(1)}, f32[1024,256]{1,0:T(8,128)}, u32[]{:S(2)}) copy-start(f32[1024,256]{1,0:T(8,128)} %copy-done.12) | copy-start | bytes 3145732
  1067.3 18.1 %copy-start.33 = (f32[2,1024,256]{2,1,0:T(8,128)S(1)}, f32[2,1024,256]{2,1,0:T(8,128)}, u32[]{:S(2)}) copy-start(f32[2,1024,256]{2,1,0:T(8,128)} %reduce-scatter.23.cloned.1.call-done) | copy-start | bytes 6291460
  1085.3 40.8 %copy-start.53 = (f32[1024]{0:T(1024)S(1)}, f32[1024]{0:T(1024)}, u32[]{:S(2)}) copy-start(f32[1024]{0:T(1024)} %copy-done.52) | copy-start | bytes 12292
  1085.3 40.8 %copy-start.7 = (f32[2,1024,256]{2,1,0:T(8,128)S(1)}, f32[2,1024,256]{2,1,0:T(8,128)}, u32[]{:S(2)}) copy-start(f32[2,1024,256]{2,1,0:T(8,128)} %reduce-scatter.15.cloned.1.call-done) | copy-start | bytes 6291460
  1085.3 40.8 %copy-start.18 = (bf16[1,1024,256]{2,1,0:T(8,128)(2,1)S(1)}, bf16[1,1024,256]{2,1,0:T(8,128)(2,1)}, u32[]{:S(2)}) copy-start(bf16[1,1024,256]{2,1,0:T(8,128)(2,1)} %param.31) | copy-start | bytes 1572868
  1085.4 40.8 %copy-start.41 = (f32[1024]{0:T(1024)S(1)}, f32[1024]{0:T(1024)}, u32[]{:S(2)}) copy-start(f32[1024]{0:T(1024)} %copy-done.40) | copy-start | bytes 12292
  1085.4 40.8 %copy-start.51 = (f32[1024]{0:T(1024)S(1)}, f32[1024]{0:T(1024)}, u32[]{:S(2)}) copy-start(f32[1024]{0:T(1024)} %copy-done.50) | copy-start | bytes 12292
  1085.4 40.8 %copy-start.63 = (f32[256]{0:T(256)S(1)}, f32[256]{0:T(256)}, u32[]{:S(2)}) copy-start(f32[256]{0:T(256)} %param.37) | copy-start | bytes 3076
  (55 other events, 275.8 us)
Sparse Core Ops, SparseCore 0:
  9.6 24.7 all-gather.16
  171.7 51.9 all-gather.12
  228.8 10.5 all-gather.18
  240.9 26.4 all-gather.14
  268.9 22.9 all-gather.20
  310.0 86.1 reduce-scatter.14
  397.8 29.0 all-gather.24
  429.5 34.6 all-gather.22
  466.2 35.1 all-gather.28
  502.9 30.8 all-gather.26
  546.3 51.7 reduce-scatter.18
  600.8 52.6 reduce-scatter.16
  658.2 52.5 all-gather.30
  744.3 8.5 reduce-scatter.24
  755.0 13.1 reduce-scatter.20
  771.5 53.9 all-reduce.3
  828.7 86.3 reduce-scatter.22
  917.9 49.9 reduce-scatter.40
  970.7 48.1 reduce-scatter.38
  1021.6 30.4 reduce-scatter.32
  1055.0 30.5 reduce-scatter.36
  1088.5 34.1 reduce-scatter.34
  1125.6 34.6 reduce-scatter.30
  1162.9 29.4 reduce-scatter.26
  1195.3 33.9 reduce-scatter.28
where the time goes:
time: 1250 us; the launch traced here: 1240 us
  waiting for transfers between devices  593 us (47%)
  matrix products  207 us (17%)
  local copies, waits for them, and re-layouts  162 us (13%)
  other arithmetic  129 us (10%)
  blocking collectives  124 us (10%)
  between operations  16 us (1%)
    reduce_scatter x2, waiting for transfers between devices, sum_features(): return lax.psum_scatter(stacked, 'tp', scatter_dimension=2, tiled=True)  130 us
    reduce_scatter x2, waiting for transfers between devices, sum_grads(): return lax.psum_scatter(stacked, 'tp', scatter_dimension=2, tiled=True)  106 us
    all_gather x2, waiting for transfers between devices, gather_features(): return lax.all_gather(stacked, 'tp', axis=2, tiled=True)  89.2 us
    all_gather x2, waiting for transfers between devices, gather_grads(): return lax.all_gather(stacked, 'tp', axis=2, tiled=True)  83 us
    dot_general x16, matrix products, one_block(): jnp.dot(linked, block_in * falling, precision=lax.Precision.HIGHEST, pref...  81.6 us
    dot_general x14, matrix products, multiply_left(): lax.dot_general(left_side, right_side, (((0,), (0,)), ((), ())), preferre...  42.2 us
    dot_general x14, matrix products, multiply_right(): lax.dot_general(left_side, right_side, (((1,), (1,)), ((), ())), preferre...  42 us
    dot_general x14, matrix products, multiply(): return jnp.dot(left_side, right_side, preferred_element_type=jnp.float32)  41.2 us
  transfers between devices with their start and end apart: 25, of which 16 were waited for; matrix products, arithmetic and copies ran while one was open for 34% of the time, Pallas kernels for 0%

commit v1 on v0

v1 whole, which is shorter than its diff:
```python
import functools
import math

import jax
import jax.numpy as jnp
from jax import lax
from jax.experimental import pallas as pl
from jax.experimental.pallas import tpu as pltpu
from jax.sharding import PartitionSpec as P

D = 1024
Z = 128
EPSILON = 1e-06
MESH = pl.DeviceIdType.MESH
F32 = jnp.float32
BF16 = jnp.bfloat16
VMEM = pl.BlockSpec(memory_space=pltpu.VMEM)
HIGH = lax.Precision.HIGHEST


def spot(f=None, c=None, t=None):
    return (
        lax.axis_index("fsdp") if f is None else f,
        lax.axis_index("ctx") if c is None else c,
        lax.axis_index("tp") if t is None else t,
    )


def greet(devices):
    barrier = pltpu.get_barrier_semaphore()
    for device in devices:
        pl.semaphore_signal(barrier, inc=1, device_id=device, device_id_type=MESH)
    pl.semaphore_wait(barrier, len(devices))


def tp_peers():
    t = lax.axis_index("tp")
    return t, t + 1 - 2 * (t % 2), (t + 2) % 4, 3 - t


def remote(src, dst, send, recv, device):
    return pltpu.make_async_remote_copy(
        src_ref=src, dst_ref=dst, send_sem=send, recv_sem=recv, device_id=device, device_id_type=MESH
    )


class Gather:
    def __init__(self, count, source, place, send, recv, base=0):
        self.count, self.half = count, count // 2
        self.source, self.place, self.send, self.recv, self.base = source, place, send, recv, base
        self.t, self.x, self.y, _ = tp_peers()

    def copy(self, src, owner, i, way, to):
        n = self.base + way * self.count + i
        return remote(src, self.place(owner, i), self.send.at[n], self.recv.at[n], spot(t=to))

    def first(self, i, way):
        return self.copy(self.source(i), self.t, i, way, self.x if way == 0 else self.y)

    def start(self):
        for k in range(self.half):
            self.first(k, 0).start()
            self.first(k + self.half, 1).start()
        for k in range(self.half):
            self.first(k + self.half, 0).start()
            self.first(k, 1).start()

    def onward(self, i):
        if i < self.half:
            return self.copy(self.place(self.x, i), self.x, i, 2, self.y)
        return self.copy(self.place(self.y, i), self.y, i, 2, self.x)

    def forward(self):
        for k in range(self.half):
            self.first(k, 0).wait_recv()
            self.onward(k).start()
            self.first(k + self.half, 1).wait_recv()
            self.onward(k + self.half).start()

    def finish(self):
        for k in range(self.half):
            self.first(k + self.half, 0).wait_recv()
            self.first(k, 1).wait_recv()
        for i in range(self.count):
            self.onward(i).wait()
            self.first(i, 0).wait_send()
            self.first(i, 1).wait_send()


def gather_kernel(arrays, chunks, *refs):
    sources, places = refs[:arrays], refs[arrays : 2 * arrays]
    send, recv = refs[2 * arrays :]
    t, x, y, d = tp_peers()
    greet([spot(t=x), spot(t=y)])
    runs = []
    for k, (src, dst) in enumerate(zip(sources, places)):
        rows, width = src.shape
        size = rows // chunks
        runs.append(
            Gather(
                chunks,
                lambda i, src=src, size=size: src.at[pl.ds(i * size, size)],
                lambda o, i, dst=dst, size=size, width=width: dst.at[
                    pl.ds(i * size, size), pl.ds(pl.multiple_of(o * width, width), width)
                ],
                send,
                recv,
                3 * chunks * k,
            )
        )
    for run in runs:
        run.start()
    for src, dst in zip(sources, places):
        width = src.shape[1]
        for o in range(4):

            @pl.when(t == o)
            def _():
                dst[:, o * width : (o + 1) * width] = src[...]

    for run in runs:
        run.forward()
    for run in runs:
        run.finish()


def tp_gather(ident, *arrays):
    chunks = 8
    n = 3 * chunks * len(arrays)
    return pl.pallas_call(
        functools.partial(gather_kernel, len(arrays), chunks),
        out_shape=[jax.ShapeDtypeStruct((a.shape[0], 4 * a.shape[1]), a.dtype) for a in arrays],
        in_specs=[VMEM] * len(arrays),
        out_specs=[VMEM] * len(arrays),
        scratch_shapes=[pltpu.SemaphoreType.DMA((n,)), pltpu.SemaphoreType.DMA((n,))],
        compiler_params=pltpu.CompilerParams(
            collective_id=ident, has_side_effects=True, vmem_limit_bytes=48 * 2**20
        ),
        name="tp_gather",
    )(*arrays)


class Scatter:
    def __init__(self, count, part, first_diag, first_own, second, send, recv, base=0):
        self.count, self.part = count, part
        self.diag, self.own, self.second = first_diag, first_own, second
        self.send, self.recv, self.base = send, recv, base
        self.t, self.x, self.y, self.d = tp_peers()

    def ways(self, i):
        return (self.x, self.y) if i % 2 == 0 else (self.y, self.x)

    def copy(self, i, kind):
        near, far = self.ways(i)
        n = self.base + kind * self.count + i
        if kind == 0:
            src, dst, to = self.part(self.d, i), self.diag(i), near
        elif kind == 1:
            src, dst, to = self.part(near, i), self.own(i), near
        else:
            src, dst, to = self.part(far, i), self.second(i), far
        return remote(src, dst, self.send.at[n], self.recv.at[n], spot(t=to))

    def start(self):
        for i in range(self.count):
            self.copy(i, 0).start()
        for i in range(self.count):
            self.copy(i, 1).start()

    def forward(self):
        for i in range(self.count):
            self.copy(i, 0).wait_recv()
            mine = self.part(self.ways(i)[1], i)
            mine[...] = (mine[...].astype(F32) + self.diag(i)[...].astype(F32)).astype(BF16)
            self.copy(i, 2).start()

    def collect(self, i):
        self.copy(i, 1).wait_recv()
        self.copy(i, 2).wait_recv()
        return self.own(i)[...].astype(F32) + self.second(i)[...].astype(F32)

    def finish(self):
        for i in range(self.count):
            for kind in range(3):
                self.copy(i, kind).wait_send()


def scatter_kernel(arrays, chunks, *refs):
    sources, outs = refs[:arrays], refs[arrays : 2 * arrays]
    part = refs[2 * arrays : 3 * arrays]
    diag, own, second, send, recv = refs[3 * arrays :]
    t, x, y, d = tp_peers()
    for k in range(arrays):
        width = outs[k].shape[1]
        for o in range(4):
            part[k][o] = sources[k][:, o * width : (o + 1) * width]
    greet([spot(t=x), spot(t=y)])
    runs = []
    for k in range(arrays):
        size = outs[k].shape[0] // chunks
        runs.append(
            Scatter(
                chunks,
                lambda o, i, k=k, size=size: part[k].at[o, pl.ds(i * size, size)],
                lambda i, k=k: diag.at[k * chunks + i],
                lambda i, k=k: own.at[k * chunks + i],
                lambda i, k=k: second.at[k * chunks + i],
                send,
                recv,
                3 * chunks * k,
            )
        )
    for run in runs:
        run.start()
    for run in runs:
        run.forward()
    for k, run in enumerate(runs):
        size = outs[k].shape[0] // chunks
        for i in range(chunks):
            outs[k][i * size : (i + 1) * size] = run.collect(i) + run.part(t, i)[...].astype(F32)
    for run in runs:
        run.finish()


def tp_scatter(ident, *arrays):
    chunks = 8
    k = len(arrays)
    n = 3 * chunks * k
    rows, width = arrays[0].shape[0], arrays[0].shape[1] // 4
    block = pltpu.VMEM((k * chunks, rows // chunks, width), BF16)
    return pl.pallas_call(
        functools.partial(scatter_kernel, k, chunks),
        out_shape=[jax.ShapeDtypeStruct((rows, width), F32) for a in arrays],
        in_specs=[VMEM] * k,
        out_specs=[VMEM] * k,
        scratch_shapes=[pltpu.VMEM((4, rows, width), BF16)] * k
        + [block, block, block, pltpu.SemaphoreType.DMA((n,)), pltpu.SemaphoreType.DMA((n,))],
        compiler_params=pltpu.CompilerParams(
            collective_id=ident, has_side_effects=True, vmem_limit_bytes=48 * 2**20
        ),
        name="tp_scatter",
    )(*arrays)


def swap_kernel(arrays, *refs):
    sources, outs = refs[:arrays], refs[arrays : 2 * arrays]
    send, recv = refs[2 * arrays :]
    other = spot(c=1 - lax.axis_index("ctx"))
    greet([other])
    copies = [
        remote(src, dst, send.at[k], recv.at[k], other)
        for k, (src, dst) in enumerate(zip(sources, outs))
    ]
    for copy in copies:
        copy.start()
    for copy in copies:
        copy.wait()


def core_swap(ident, *arrays):
    k = len(arrays)
    return pl.pallas_call(
        functools.partial(swap_kernel, k),
        out_shape=[jax.ShapeDtypeStruct(a.shape, a.dtype) for a in arrays],
        in_specs=[VMEM] * k,
        out_specs=[VMEM] * k,
        scratch_shapes=[pltpu.SemaphoreType.DMA((k,)), pltpu.SemaphoreType.DMA((k,))],
        compiler_params=pltpu.CompilerParams(
            collective_id=ident, has_side_effects=True, vmem_limit_bytes=48 * 2**20
        ),
        name="core_swap",
    )(*arrays)


def shard_at(ref, kind, index, size):
    if kind == "row":
        return ref.at[pl.ds(pl.multiple_of(index * size, size), size)]
    return ref.at[:, pl.ds(pl.multiple_of(index * size, size), size)]


def turned(kind, size):
    return kind == "col" and size % 128 != 0


def weights_kernel(kinds, sizes, count, *refs):
    k = len(kinds)
    sources, outs = refs[:k], refs[k : 2 * k]
    here, send_up, send_down, send_core, recv, recv_core = refs[2 * k :]
    z, c = lax.axis_index("fsdp"), lax.axis_index("ctx")
    other = spot(c=1 - c)
    up, down = spot(f=(z + 1) % count), spot(f=(z + count - 1) % count)
    greet([other, up, down])

    def slot(w, owner, core):
        return shard_at(outs[w], kinds[w], owner * 2 + core, sizes[w])

    def to_core(w, owner, src):
        return remote(src, slot(w, owner, c), send_core.at[w, owner], recv_core.at[w, owner], other)

    def to_up(w, owner, src):
        return remote(src, slot(w, owner, c), send_up.at[w, owner], recv.at[w, owner], up)

    def to_down(w, owner, src):
        return remote(src, slot(w, owner, c), send_down.at[w, owner], recv.at[w, owner], down)

    def keep(w):
        return pltpu.make_async_copy(sources[w], slot(w, z, c), here.at[w])

    for w in range(k):

        @pl.when(z + 1 < count)
        def _():
            to_up(w, z, sources[w]).start()

        @pl.when(z > 0)
        def _():
            to_down(w, z, sources[w]).start()

        to_core(w, z, sources[w]).start()
        keep(w).start()

    @pl.loop(1, count)
    def _(step):
        for w in range(k):
            low, high = z - step, z + step

            @pl.when(low >= 0)
            def _():
                got = slot(w, low, c)
                to_up(w, low, got).wait_recv()

                @pl.when(z + 1 < count)
                def _():
                    to_up(w, low, got).start()

                to_core(w, low, got).start()

            @pl.when(high < count)
            def _():
                got = slot(w, high, c)
                to_down(w, high, got).wait_recv()

                @pl.when(z > 0)
                def _():
                    to_down(w, high, got).start()

                to_core(w, high, got).start()

    @pl.loop(0, count)
    def _(owner):
        for w in range(k):
            got = slot(w, owner, c)
            to_core(w, owner, got).wait()

            @pl.when((owner <= z) & (z + 1 < count))
            def _():
                to_up(w, owner, got).wait_send()

            @pl.when((owner >= z) & (z > 0))
            def _():
                to_down(w, owner, got).wait_send()

    for w in range(k):
        keep(w).wait()


def weights_gather(ident, count, kinds, shards):
    turns = [turned(k, s.shape[1]) for k, s in zip(kinds, shards)]
    shards = [s.T if turn else s for turn, s in zip(turns, shards)]
    kinds = ["row" if turn else k for turn, k in zip(turns, kinds)]
    sizes = [s.shape[0] if k == "row" else s.shape[1] for k, s in zip(kinds, shards)]
    outs = []
    for kind, size, s in zip(kinds, sizes, shards):
        shape = (2 * count * size, s.shape[1]) if kind == "row" else (s.shape[0], 2 * count * size)
        outs.append(jax.ShapeDtypeStruct(shape, s.dtype))
    k = len(shards)
    dma = pltpu.SemaphoreType.DMA
    got = pl.pallas_call(
        functools.partial(weights_kernel, kinds, sizes, count),
        out_shape=outs,
        in_specs=[VMEM] * k,
        out_specs=[VMEM] * k,
        scratch_shapes=[dma((k,))] + [dma((k, count))] * 5,
        compiler_params=pltpu.CompilerParams(
            collective_id=ident, has_side_effects=True, vmem_limit_bytes=48 * 2**20
        ),
        name="weights_gather",
    )(*shards)
    return [g.T if turn else g for turn, g in zip(turns, got)]


def grads_kernel(kinds, sizes, count, *refs):
    k = len(kinds)
    sources, outs = refs[:k], refs[k : 2 * k]
    pair, line = refs[2 * k : 3 * k], refs[3 * k : 4 * k]
    send_core, recv_core, send, recv = refs[4 * k :]
    z, c = lax.axis_index("fsdp"), lax.axis_index("ctx")
    other = spot(c=1 - c)
    up, down = spot(f=(z + 1) % count), spot(f=(z + count - 1) % count)
    greet([other, up, down])

    def block(w, owner, core):
        return shard_at(sources[w], kinds[w], owner * 2 + core, sizes[w])

    def to_core(w, owner):
        return remote(
            block(w, owner, 1 - c), pair[w].at[owner], send_core.at[w, owner], recv_core.at[w, owner], other
        )

    def to_up(w, owner):
        return remote(pair[w].at[owner], line[w].at[owner], send.at[w, owner], recv.at[w, owner], up)

    def to_down(w, owner):
        at = jnp.where(owner == z - 1, count, owner)
        return remote(pair[w].at[owner], line[w].at[at], send.at[w, owner], recv.at[w, at], down)

    def arrived(w, at):
        remote(pair[w].at[0], line[w].at[at], send.at[w, 0], recv.at[w, at], up).wait_recv()

    def plus(w, owner):
        return pair[w][owner].astype(F32) + block(w, owner, c)[...].astype(F32)

    @pl.loop(0, count)
    def _(i):
        for w in range(k):
            to_core(w, count - 1 - i).start()

    @pl.loop(0, count)
    def _(i):
        for w in range(k):
            for owner, going_up in ((count - 1 - i, True), (i, False)):

                @pl.when(owner > z if going_up else owner < z)
                def _():
                    to_core(w, owner).wait_recv()
                    total = plus(w, owner)
                    pair[w][owner] = total.astype(BF16)

                    @pl.when(z > 0 if going_up else z + 1 < count)
                    def _():
                        arrived(w, owner)
                        pair[w][owner] = (total + line[w][owner].astype(F32)).astype(BF16)

                    (to_up if going_up else to_down)(w, owner).start()

    for w in range(k):
        to_core(w, z).wait_recv()
        outs[w][...] = plus(w, z)

        @pl.when(z > 0)
        def _():
            arrived(w, z)
            outs[w][...] += line[w][z].astype(F32)

        @pl.when(z + 1 < count)
        def _():
            arrived(w, count)
            outs[w][...] += line[w][count].astype(F32)

    @pl.loop(0, count)
    def _(owner):
        for w in range(k):
            to_core(w, owner).wait_send()

            @pl.when(owner > z)
            def _():
                to_up(w, owner).wait_send()

            @pl.when(owner < z)
            def _():
                to_down(w, owner).wait_send()


def grads_scatter(ident, count, kinds, grads):
    grads = [g.astype(BF16) for g in grads]
    turns = [turned(k, g.shape[1] // (2 * count)) for k, g in zip(kinds, grads)]
    grads = [g.T if turn else g for turn, g in zip(turns, grads)]
    kinds = ["row" if turn else k for turn, k in zip(turns, kinds)]
    sizes = [g.shape[0 if k == "row" else 1] // (2 * count) for k, g in zip(kinds, grads)]
    blocks = [
        (s, g.shape[1]) if k == "row" else (g.shape[0], s) for k, s, g in zip(kinds, sizes, grads)
    ]
    k = len(grads)
    dma = pltpu.SemaphoreType.DMA
    got = pl.pallas_call(
        functools.partial(grads_kernel, kinds, sizes, count),
        out_shape=[jax.ShapeDtypeStruct(b, F32) for b in blocks],
        in_specs=[VMEM] * k,
        out_specs=[VMEM] * k,
        scratch_shapes=[pltpu.VMEM((count,) + b, BF16) for b in blocks]
        + [pltpu.VMEM((count + 1,) + b, BF16) for b in blocks]
        + [dma((k, count)), dma((k, count)), dma((k, count)), dma((k, count + 1))],
        compiler_params=pltpu.CompilerParams(
            collective_id=ident, has_side_effects=True, vmem_limit_bytes=48 * 2**20
        ),
        name="grads_scatter",
    )(*grads)
    return [g.T if turn else g for turn, g in zip(turns, got)]


def row_exchange(rows, send, recv):
    t, x, y, d = tp_peers()
    return [
        remote(rows.at[t], rows.at[t], send.at[k], recv.at[k], spot(t=p))
        for k, p in enumerate((x, y, d))
    ]


def row_sums(values):
    return lax.dot_general(
        jnp.ones((8, values.shape[1]), F32),
        values,
        (((1,), (1,)), ((), ())),
        precision=HIGH,
        preferred_element_type=F32,
    )


def tree_sum(terms):
    while len(terms) > 1:
        terms = [a + b for a, b in zip(terms[::2], terms[1::2])]
    return terms[0]


def wide(row):
    return jnp.broadcast_to(row, (8, 128))


def power(base, exponent):
    result, square = None, base
    while exponent:
        if exponent & 1:
            result = square if result is None else result * square
        exponent >>= 1
        if exponent:
            square = square * square
    return result


def front_kernel(
    tok, keep, gain, damp, eta,
    normed4, mixed4, mix_pre, xn, inv_out,
    low_n, low_m, rows, ends, starts, end_out, end_in,
    send, recv, row_send, row_recv, core_send, core_recv,
):
    t, x, y, d = tp_peers()
    c = lax.axis_index("ctx")
    other = spot(c=1 - c)
    groups, count = xn.shape[0], xn.shape[1]
    step, nj = count // 8, damp.shape[0]
    end_in[...] = jnp.zeros_like(end_in)
    value = tok[...].astype(F32)
    rows[t] = row_sums(value * value)
    greet([spot(t=x), spot(t=y), spot(t=d), other])
    sums = row_exchange(rows, row_send, row_recv)
    for copy in sums:
        copy.start()
    for copy in sums:
        copy.wait()
    inv = lax.rsqrt((rows[0] + rows[1] + rows[2] + rows[3]) / D + EPSILON)
    inv_out[...] = inv
    normed = tok[...].astype(F32) * inv.T[:, 0:1] * gain[...]
    low_n[...] = normed.astype(BF16)
    for g in range(groups):
        xn[g] = normed[:, g * 128 : (g + 1) * 128]
    width = groups * 128
    chunks = 8
    size = count // chunks
    first = Gather(
        chunks,
        lambda i: low_n.at[pl.ds(i * size, size)],
        lambda o, i: normed4.at[pl.ds(i * size, size), pl.ds(pl.multiple_of(o * width, width), width)],
        send, recv, 0,
    )
    halves = [
        Gather(
            4,
            lambda i, g=g: low_m.at[pl.ds(i * 2 * size, 2 * size), pl.ds(g * 128, 128)],
            lambda o, i, g=g: mixed4.at[
                pl.ds(i * 2 * size, 2 * size), pl.ds(pl.multiple_of(o * width + g * 128, 128), 128)
            ],
            send, recv, 24 + 12 * g,
        )
        for g in range(groups)
    ]
    first.start()

    for g in range(groups):
        ln = pl.ds(g * 128, 128)
        decay = [wide(1.0 - damp[pl.ds(j, 1), ln]) for j in range(nj)]

        def scan(s, carry):
            states, chain = carry
            at = pl.ds(s, 8, stride=step)
            v, k = xn[g, at, :], keep[at, :]
            return tuple(v + (k * r) * a for r, a in zip(decay, states)), chain * k

        zero = jnp.zeros((8, 128), F32)
        states, chain = lax.fori_loop(0, step, scan, ((zero,) * nj, zero + 1.0), unroll=4)
        for j in range(nj):
            ends[0, j, :, ln] = states[j]
            ends[1, j, :, ln] = power(decay[j], step) * chain

    last = jnp.zeros((nj, width), F32)
    for q in range(8):
        last = ends[0, :, q, :] + ends[1, :, q, :] * last
    end_out[...] = last
    across = remote(end_out, end_in, core_send.at[0], core_recv.at[0], other)
    across.start()
    across.wait()
    last = jnp.where(c == 0, 0.0, end_in[...])
    for q in range(8):
        starts[:, q, :] = last
        last = ends[0, :, q, :] + ends[1, :, q, :] * last

    for g in range(groups):
        ln = pl.ds(g * 128, 128)
        decay = [wide(1.0 - damp[pl.ds(j, 1), ln]) for j in range(nj)]
        weight = [wide(damp[pl.ds(j, 1), ln] * eta[pl.ds(j, 1), ln]) for j in range(nj)]

        def scan(s, states):
            at = pl.ds(s, 8, stride=step)
            v, k = xn[g, at, :], keep[at, :]
            states = tuple(v + (k * r) * a for r, a in zip(decay, states))
            mix_pre[g, at, :] = v + tree_sum([w * a for w, a in zip(weight, states)])
            return states

        lax.fori_loop(0, step, scan, tuple(starts[j, :, ln] for j in range(nj)), unroll=4)
        pre = mix_pre[g]
        low_m[:, ln] = (pre * jax.nn.sigmoid(pre)).astype(BF16)
        halves[g].start()
    for o in range(4):

        @pl.when(t == o)
        def _():
            normed4[:, o * width : (o + 1) * width] = low_n[...]
            mixed4[:, o * width : (o + 1) * width] = low_m[...]

    first.forward()
    for run in halves:
        run.forward()
    for run in [first] + halves:
        run.finish()


def front(ident, tok, keep, gain, damp, eta):
    count, width = tok.shape
    groups, nj = width // 128, damp.shape[0]
    dma = pltpu.SemaphoreType.DMA
    lanes = jax.ShapeDtypeStruct((groups, count, 128), F32)
    full = jax.ShapeDtypeStruct((count, 4 * width), BF16)
    n = 24 + 12 * groups
    return pl.pallas_call(
        front_kernel,
        out_shape=[full, full, lanes, lanes, jax.ShapeDtypeStruct((8, count), F32)],
        in_specs=[VMEM] * 5,
        out_specs=[VMEM] * 5,
        scratch_shapes=[
            pltpu.VMEM((count, width), BF16),
            pltpu.VMEM((count, width), BF16),
            pltpu.VMEM((4, 8, count), F32),
            pltpu.VMEM((2, nj, 8, width), F32),
            pltpu.VMEM((nj, 8, width), F32),
            pltpu.VMEM((nj, width), F32),
            pltpu.VMEM((nj, width), F32),
            dma((n,)), dma((n,)), dma((3,)), dma((3,)), dma((1,)), dma((1,)),
        ],
        compiler_params=pltpu.CompilerParams(
            collective_id=ident, has_side_effects=True, vmem_limit_bytes=48 * 2**20
        ),
        name="front",
    )(tok, keep, gain[None], damp, eta)


def tail_kernel(
    mix_sum, value_sum, mix_pre, xn, tok, inv_in, keep_next, gain, damp, eta, tok_part,
    grad_in, gain_grad, eta_grad, damp_grad,
    grad_mix, back, rows, ends, starts, end_out, end_in,
    row_send, row_recv, core_send, core_recv,
):
    t, x, y, d = tp_peers()
    c = lax.axis_index("ctx")
    other = spot(c=1 - c)
    groups, count = xn.shape[0], xn.shape[1]
    step, nj, width = count // 8, damp.shape[0], damp.shape[1]
    part = 8
    zero = jnp.zeros((8, 128), F32)
    end_in[...] = jnp.zeros_like(end_in)
    for g in range(groups):
        pre = mix_pre[g]
        sig = jax.nn.sigmoid(pre)
        grad_mix[g] = mix_sum[:, g * 128 : (g + 1) * 128] * (sig * (1.0 + pre * (1.0 - sig)))
    greet([spot(t=x), spot(t=y), spot(t=d), other])

    for g in range(groups):
        ln = pl.ds(g * 128, 128)
        for j0 in range(0, nj, part):
            decay = [wide(1.0 - damp[pl.ds(j, 1), ln]) for j in range(j0, j0 + part)]

            def scan(i, carry):
                a, w, chain = carry
                at = pl.ds(step - 1 - i, 8, stride=step)
                v, k = grad_mix[g, at, :], keep_next[at, :]
                held = [k * r for r in decay]
                w = tuple(k * p + r * q for p, r, q in zip(a, held, w))
                a = tuple(v + r * p for r, p in zip(held, a))
                return a, w, chain * k

            a, w, chain = lax.fori_loop(
                0, step, scan, ((zero,) * part, (zero,) * part, zero + 1.0), unroll=4
            )
            for n in range(part):
                less = power(decay[n], step - 1)
                ends[0, j0 + n, :, ln] = a[n]
                ends[1, j0 + n, :, ln] = w[n]
                ends[2, j0 + n, :, ln] = less * decay[n] * chain
                ends[3, j0 + n, :, ln] = float(step) * less * chain

    def merge(q, a, w):
        return (
            ends[0, :, q, :] + ends[2, :, q, :] * a,
            ends[1, :, q, :] + ends[2, :, q, :] * w + ends[3, :, q, :] * a,
        )

    a = w = jnp.zeros((nj, width), F32)
    for q in range(7, -1, -1):
        a, w = merge(q, a, w)
    end_out[0] = a
    end_out[1] = w
    across = remote(end_out, end_in, core_send.at[0], core_recv.at[0], other)
    across.start()
    across.wait()
    a, w = jnp.where(c == 0, end_in[0], 0.0), jnp.where(c == 0, end_in[1], 0.0)
    for q in range(7, -1, -1):
        starts[0, :, q, :] = a
        starts[1, :, q, :] = w
        a, w = merge(q, a, w)

    for g in range(groups):
        ln = pl.ds(g * 128, 128)
        for j0 in range(0, nj, part):
            span = range(j0, j0 + part)
            decay = [wide(1.0 - damp[pl.ds(j, 1), ln]) for j in span]
            weight = [wide(damp[pl.ds(j, 1), ln] * eta[pl.ds(j, 1), ln]) for j in span]

            def scan(i, carry):
                a, w, sum_a, sum_w = carry
                at = pl.ds(step - 1 - i, 8, stride=step)
                v, k, u = grad_mix[g, at, :], keep_next[at, :], xn[g, at, :]
                held = [k * r for r in decay]
                w = tuple(k * p + r * q for p, r, q in zip(a, held, w))
                a = tuple(v + r * p for r, p in zip(held, a))
                sum_a = tuple(s + u * p for s, p in zip(sum_a, a))
                sum_w = tuple(s + u * p for s, p in zip(sum_w, w))
                base = v if j0 == 0 else back[g, at, :]
                back[g, at, :] = base + tree_sum([r * p for r, p in zip(weight, a)])
                return a, w, sum_a, sum_w

            first = (tuple(starts[0, j, :, ln] for j in span), tuple(starts[1, j, :, ln] for j in span))
            _, _, sum_a, sum_w = lax.fori_loop(
                0, step, scan, first + ((zero,) * part, (zero,) * part), unroll=4
            )
            for n, j in enumerate(span):
                at = pl.ds(j, 1)
                all_a = jnp.sum(sum_a[n], axis=0, keepdims=True)
                all_w = jnp.sum(sum_w[n], axis=0, keepdims=True)
                rate = damp[at, ln]
                eta_grad[at, ln] = rate * all_a
                damp_grad[at, ln] = eta[at, ln] * (all_a - rate * all_w)

    inv = inv_in[...].T[:, 0:1]
    value = tok[...].astype(F32)
    back_all = jnp.concatenate([back[g] for g in range(groups)], axis=1)
    grad_normed = value_sum[...] + back_all
    gain_grad[...] = jnp.sum(grad_normed * value * inv, axis=0, keepdims=True)
    scaled = grad_normed * gain[...]
    rows[t] = row_sums(scaled * value)
    sums = row_exchange(rows, row_send, row_recv)
    for copy in sums:
        copy.start()
    grad_in[...] = tok_part[...] + inv * scaled
    for copy in sums:
        copy.wait()
    factor = inv_in[...]
    factor = factor * factor * factor * (rows[0] + rows[1] + rows[2] + rows[3]) / D
    grad_in[...] -= value * factor.T[:, 0:1]


def tail(ident, mix_sum, value_sum, mix_pre, xn, tok, inv_in, keep_next, gain, damp, eta, tok_part):
    count, width = tok.shape
    groups, nj = width // 128, damp.shape[0]
    dma = pltpu.SemaphoreType.DMA
    small = jax.ShapeDtypeStruct((nj, width), F32)
    return pl.pallas_call(
        tail_kernel,
        out_shape=[
            jax.ShapeDtypeStruct((count, width), F32),
            jax.ShapeDtypeStruct((1, width), F32),
            small,
            small,
        ],
        in_specs=[VMEM] * 11,
        out_specs=[VMEM] * 4,
        scratch_shapes=[
            pltpu.VMEM((groups, count, 128), F32),
            pltpu.VMEM((groups, count, 128), F32),
            pltpu.VMEM((4, 8, count), F32),
            pltpu.VMEM((4, nj, 8, width), F32),
            pltpu.VMEM((2, nj, 8, width), F32),
            pltpu.VMEM((2, nj, width), F32),
            pltpu.VMEM((2, nj, width), F32),
            dma((3,)), dma((3,)), dma((1,)), dma((1,)),
        ],
        compiler_params=pltpu.CompilerParams(
            collective_id=ident, has_side_effects=True, vmem_limit_bytes=48 * 2**20
        ),
        name="tail",
    )(mix_sum, value_sum, mix_pre, xn, tok, inv_in, keep_next, gain[None], damp, eta, tok_part)


def multiply(left_side, right_side):
    return jnp.dot(left_side, right_side, preferred_element_type=F32)


def multiply_left(left_side, right_side):
    return lax.dot_general(
        left_side, right_side, (((0,), (0,)), ((), ())), preferred_element_type=F32
    )


def multiply_right(left_side, right_side):
    return lax.dot_general(
        left_side, right_side, (((1,), (1,)), ((), ())), preferred_element_type=F32
    )


def silu_grad(pre_act):
    sigmoid_pre = jax.nn.sigmoid(pre_act)
    return sigmoid_pre * (1.0 + pre_act * (1.0 - sigmoid_pre))


KINDS = ("row", "row", "row", "col", "col", "col", "row", "col")


def on_device(
    line_count,
    layer_input, segment_ids, cotangent, norm_gain, ema_damping, ema_eta, query_gain, key_gain,
    ffn_gain, *weights,
):
    tok = layer_input[0]
    tokens = tok.astype(F32)
    segment = segment_ids[0]
    row_count, local_dim = tok.shape
    core = lax.axis_index("ctx")
    offset = core * row_count
    all_ids = lax.all_gather(segment, "ctx", axis=0, tiled=True)
    key_count = all_ids.shape[0]
    same = jnp.concatenate(
        [jnp.zeros((1,), F32), (all_ids[1:] == all_ids[:-1]).astype(F32), jnp.zeros((1,), F32)]
    )
    keep = lax.dynamic_slice_in_dim(same, offset, row_count, 0)
    keep_next = lax.dynamic_slice_in_dim(same, offset + 1, row_count, 0)
    keep_wide = jnp.broadcast_to(keep[:, None], (row_count, 128))
    next_wide = jnp.broadcast_to(keep_next[:, None], (row_count, 128))

    (
        full_shared, full_value, full_gate, full_hidden, full_attended, full_update, full_up, full_down,
    ) = weights_gather(1, line_count, KINDS, weights)
    normed_full, mixed_full, mix_pre, xn, inv_in = front(2, tok, keep_wide, norm_gain, ema_damping, ema_eta)
    mixed_low = lax.dynamic_slice_in_dim(mixed_full, lax.axis_index("tp") * local_dim, local_dim, 1)

    shared_pre = multiply(mixed_full, full_shared)
    shared = jax.nn.silu(shared_pre)
    queries = (shared * query_gain[None]).astype(BF16)
    key_rows = (shared * key_gain[None]).astype(BF16)
    value_pre = multiply(normed_full, full_value)
    values = jax.nn.silu(value_pre).astype(BF16)
    gate_pre = multiply(mixed_full, full_gate)
    gate_rows = jax.nn.silu(gate_pre)
    other_keys, other_values = core_swap(3, key_rows, values)

    def both(own, other):
        return jnp.where(core == 0, jnp.concatenate([own, other]), jnp.concatenate([other, own]))

    all_keys, all_values = both(key_rows, other_keys), both(values, other_values)
    block_size = math.gcd(row_count, 512)
    block_count = row_count // block_size
    key_position = jnp.arange(key_count)

    def block_scores(block_index):
        first_row = block_index * block_size
        query_block = lax.dynamic_slice_in_dim(queries, first_row, block_size, 0)
        ids_block = lax.dynamic_slice_in_dim(segment, first_row, block_size, 0)
        query_position = offset + first_row + jnp.arange(block_size)
        raw_scores = multiply_right(query_block, all_keys) / math.sqrt(Z)
        allowed = (query_position[:, None] >= key_position[None, :]) & (
            ids_block[:, None] == all_ids[None, :]
        )
        return (jnp.where(allowed, raw_scores, -1e30), query_block)

    def attend_block(block_index):
        scores, query_block = block_scores(block_index)
        row_peak = jnp.max(scores, axis=1, keepdims=True)
        exponent = jnp.exp(scores - row_peak)
        row_total = jnp.sum(exponent, axis=1, keepdims=True)
        probabilities = (exponent / row_total).astype(BF16)
        return (multiply(probabilities, all_values), (row_peak + jnp.log(row_total))[:, 0])

    attended_blocks, log_blocks = lax.map(attend_block, jnp.arange(block_count))
    attended = attended_blocks.reshape(row_count, -1)
    log_totals = log_blocks.reshape(row_count)
    gated_rows = (gate_rows * attended).astype(BF16)
    hidden_part = multiply(mixed_low, full_hidden) + multiply(gated_rows, full_attended)
    update_part = multiply(mixed_low, full_update)
    hidden_pre, update_pre = tp_scatter(4, hidden_part.astype(BF16), update_part.astype(BF16))
    update = jax.nn.sigmoid(update_pre)
    hidden_act = jax.nn.silu(hidden_pre)
    block_out = update * hidden_act + (1.0 - update) * tokens
    squares = lax.psum(jnp.sum(block_out * block_out, axis=1), "tp")
    inverse_mid = lax.rsqrt(squares / D + EPSILON)
    ffn_normed = block_out * inverse_mid[:, None] * ffn_gain[None]
    ffn_full, grad_full = tp_gather(5, ffn_normed.astype(BF16), cotangent[0])
    up_pre = multiply(ffn_full, full_up)
    up_rows = jax.nn.silu(up_pre).astype(BF16)
    ffn_part = multiply(up_rows, full_down)
    grad_down = multiply_left(up_rows, grad_full)
    grad_up_pre = (multiply_right(grad_full, full_down) * silu_grad(up_pre)).astype(BF16)
    grad_up = multiply_left(ffn_full, grad_up_pre)
    grad_ffn_part = multiply_right(grad_up_pre, full_up)
    ffn_out, grad_ffn_normed = tp_scatter(6, ffn_part.astype(BF16), grad_ffn_part.astype(BF16))
    result = (block_out + ffn_out).astype(BF16)
    grad_out = cotangent[0].astype(F32)
    scaled = grad_ffn_normed * ffn_gain[None]
    inner_sums = lax.psum(jnp.sum(scaled * block_out, axis=1), "tp")
    grad_mid = (
        inverse_mid[:, None] * scaled
        - block_out * (inverse_mid * inverse_mid * inverse_mid * inner_sums / D)[:, None]
    )
    grad_ffn_gain = jnp.sum(grad_ffn_normed * block_out * inverse_mid[:, None], axis=0)
    grad_block = grad_out + grad_mid
    grad_update_pre = (grad_block * (hidden_act - tokens) * update * (1.0 - update)).astype(BF16)
    grad_hidden_pre = (grad_block * update * silu_grad(hidden_pre)).astype(BF16)
    grad_tokens = grad_block * (1.0 - update)
    grad_hidden_full, grad_update_full = tp_gather(7, grad_hidden_pre, grad_update_pre)
    grad_hidden_weight = multiply_left(mixed_low, grad_hidden_full)
    grad_update_weight = multiply_left(mixed_low, grad_update_full)
    grad_attended_weight = multiply_left(gated_rows, grad_hidden_full)
    grad_gated = multiply_right(grad_hidden_full, full_attended)
    grad_mixed_local = multiply_right(grad_hidden_full, full_hidden) + multiply_right(
        grad_update_full, full_update
    )
    grad_attended = (grad_gated * gate_rows).astype(BF16)
    grad_gate_pre = (grad_gated * attended * silu_grad(gate_pre)).astype(BF16)

    def backward_block(running, block_index):
        key_sums, value_sums = running
        scores, query_block = block_scores(block_index)
        first_row = block_index * block_size
        exact = jnp.exp(
            scores - lax.dynamic_slice_in_dim(log_totals, first_row, block_size, 0)[:, None]
        )
        grad_block_out = lax.dynamic_slice_in_dim(grad_attended, first_row, block_size, 0)
        value_sums = value_sums + multiply_left(exact.astype(BF16), grad_block_out)
        grad_probs = multiply_right(grad_block_out, all_values)
        row_inner = jnp.sum(exact * grad_probs, axis=1, keepdims=True)
        grad_scores = exact * (grad_probs - row_inner) / math.sqrt(Z)
        scores_high = grad_scores.astype(BF16)
        scores_rest = (grad_scores - scores_high.astype(F32)).astype(BF16)
        grad_query_block = multiply(scores_high, all_keys) + multiply(scores_rest, all_keys)
        key_sums = (
            key_sums
            + multiply_left(scores_high, query_block)
            + multiply_left(scores_rest, query_block)
        )
        return ((key_sums, value_sums), grad_query_block)

    (key_sums, value_sums), query_blocks = lax.scan(
        backward_block,
        (
            jnp.zeros((key_count, key_rows.shape[1]), F32),
            jnp.zeros((key_count, values.shape[1]), F32),
        ),
        jnp.arange(block_count),
    )
    grad_queries = query_blocks.reshape(row_count, -1)

    def half(sums, which):
        return lax.dynamic_slice_in_dim(sums, which * row_count, row_count, 0)

    far_keys, far_values = core_swap(8, half(key_sums, 1 - core), half(value_sums, 1 - core))
    key_grads = half(key_sums, core) + far_keys
    value_grads = half(value_sums, core) + far_values
    grad_queries, key_grads = lax.psum((grad_queries, key_grads), "tp")
    grad_value_pre = (value_grads * silu_grad(value_pre)).astype(BF16)
    grad_shared = grad_queries * query_gain[None] + key_grads * key_gain[None]
    grad_query_gain = jnp.sum(shared * grad_queries, axis=0)
    grad_key_gain = jnp.sum(shared * key_grads, axis=0)
    grad_shared_pre = (grad_shared * silu_grad(shared_pre)).astype(BF16)
    grad_shared_weight = multiply_left(mixed_full, grad_shared_pre)
    grad_value_weight = multiply_left(normed_full, grad_value_pre)
    grad_gate_weight = multiply_left(mixed_full, grad_gate_pre)
    own_shared = lax.dynamic_slice_in_dim(
        full_shared, lax.axis_index("tp") * local_dim, local_dim, 0
    )
    grad_mixed_local = grad_mixed_local + multiply_right(grad_shared_pre, own_shared)
    back_value, back_gate = tp_scatter(
        9,
        multiply_right(grad_value_pre, full_value).astype(BF16),
        multiply_right(grad_gate_pre, full_gate).astype(BF16),
    )
    grad_in, grad_norm_gain, grad_eta, grad_damping = tail(
        10, grad_mixed_local + back_gate, back_value, mix_pre, xn, tok, inv_in, next_wide,
        norm_gain, ema_damping, ema_eta, grad_tokens,
    )
    small_sums = lax.psum(
        (grad_norm_gain[0], grad_damping, grad_eta, grad_query_gain, grad_key_gain, grad_ffn_gain),
        ("fsdp", "ctx"),
    )
    weight_sums = grads_scatter(
        11, line_count, KINDS,
        (
            grad_shared_weight, grad_value_weight, grad_gate_weight, grad_hidden_weight,
            grad_attended_weight, grad_update_weight, grad_up, grad_down,
        ),
    )
    return (result[None], grad_in[None], *small_sums, *weight_sums)


def solution(mesh):
    token = P("fsdp", "ctx", "tp")
    row, col = P(("fsdp", "ctx"), "tp"), P("tp", ("fsdp", "ctx"))
    shared = P(("fsdp", "ctx"), None)
    weights = (shared, row, row, col, col, col, row, col)
    small = P(None, "tp")
    return jax.shard_map(
        functools.partial(on_device, mesh.shape["fsdp"]),
        mesh=mesh,
        in_specs=(token, P("fsdp", "ctx"), token, P("tp"), small, small, P(), P(), P("tp")) + weights,
        out_specs=(token, token, P("tp"), small, small, P(), P(), P("tp")) + weights,
        check_vma=False,
    )
```

time: 1250 us -> 697 us (0.56)
  waiting for transfers between devices: 593 us -> 0.02 us
  Pallas kernels: 0 us -> 437 us
  local copies, waits for them, and re-layouts: 162 us -> 44.4 us
  other arithmetic: 129 us -> 18.2 us
  matrix products: 207 us -> 115 us
  blocking collectives: 124 us -> 54.3 us
    pallas_call x0 -> x11, Pallas kernels: none -> 437 us  [the longest x3 124 us: tp_scatter(): pl.pallas_call(functools.partial(scatter_kernel, k, chunks), out_shape=[j...]
    reduce_scatter x14 -> x0, waiting for transfers between devices: 353 us -> none  [the longest x2 130 us: sum_features(): return lax.psum_scatter(stacked, 'tp', scatter_dimension=2, tiled=True)]
    all_gather x10 -> x0, waiting for transfers between devices: 220 us -> none  [the longest x2 89.2 us: gather_features(): return lax.all_gather(stacked, 'tp', axis=2, tiled=True)]
    dot_general x30 -> x14, matrix products: 123 us -> 36.4 us  [multiply(): return jnp.dot(left_side, right_side, preferred_element_type=F32)]
    reduce_sum x7 -> x2, other arithmetic: 56.6 us -> 1.05 us  [the longest x1 0.66 us: on_device(): squares = lax.psum(jnp.sum(block_out * block_out, axis=1), 'tp')]
    all_gather x8 -> x0, blocking collectives: 53.6 us -> none  [the longest x1 15.3 us: gather_weights(): lax.all_gather(hidden_weight, ('fsdp', 'ctx'), axis=1, tiled=True)]
    mul x4 -> x0, local copies, waits for them, and re-layouts: 50.7 us -> none  [the longest x2 25.4 us: on_device(): ema_damping[None] * normed[:, None, :]]
    mul x4 -> x0, other arithmetic: 30.6 us -> none  [the longest x1 12.3 us: on_device(): ema_damping[None] * normed[:, None, :]]
  transfers between devices with their start and end apart: 25 -> 1, of which waited for: 16 -> 0; matrix products, arithmetic and copies ran while one was open for 34% -> 4% of each run, Pallas kernels for 0% -> 7%
where the time goes in v1:
time: 697 us; the launch traced here: 688 us
  Pallas kernels  437 us (63%)
  matrix products  115 us (16%)
  blocking collectives  54.3 us (8%)
  local copies, waits for them, and re-layouts  44.4 us (6%)
  other arithmetic  18.2 us (3%)
  between operations  15.5 us (2%)
    pallas_call x3, Pallas kernels, tp_scatter(): pl.pallas_call(functools.partial(scatter_kernel, k, chunks), out_shape=[j...  124 us
    pallas_call x1, Pallas kernels, grads_scatter(): pl.pallas_call(functools.partial(grads_kernel, kinds, sizes, count), out_...  86.6 us
    pallas_call x1, Pallas kernels, weights_gather(): pl.pallas_call(functools.partial(weights_kernel, kinds, sizes, count), ou...  77.2 us
    pallas_call x2, Pallas kernels, tp_gather(): pl.pallas_call(functools.partial(gather_kernel, len(arrays), chunks), out...  65.7 us
    pallas_call x1, Pallas kernels, front(): pl.pallas_call(front_kernel, out_shape=[full, full, lanes, lanes, jax.Sha...  45.2 us
    dot_general x14, matrix products, multiply_right(): lax.dot_general(left_side, right_side, (((1,), (1,)), ((), ())), preferre...  40.6 us
    dot_general x14, matrix products, multiply_left(): lax.dot_general(left_side, right_side, (((0,), (0,)), ((), ())), preferre...  38.5 us
    dot_general x14, matrix products, multiply(): return jnp.dot(left_side, right_side, preferred_element_type=F32)  36.4 us
  transfers between devices with their start and end apart: 1, of which 0 were waited for; matrix products, arithmetic and copies ran while one was open for 4% of the time, Pallas kernels for 7%

profile of v1, /device:TPU:0, one launch (start us, length us, event | category | flops | bytes accessed | tf_op | source)
XLA Modules:
  0.0 688.2 jit_solution(14546020178829780526)
XLA Ops:
  7.3 2.1 all-gather
  13.6 45.2 %front.1 = (bf16[1024,1024]{1,0:T(8,128)(2,1)S(1)}, bf16[1024,1024]{1,0:T(8,128)(2,1)}, f32[2,1024,128]{2,1,0:T(8,128)S(1)}, f32[2,1024,128]{2,1,0:T(8,128)S(1)}, f32[8,1024]{1,0:T(8,128)S(1)}) custom-call(bf16[1024,256]{1,0:T(8,128)(2,1)S(1)} %bitcast.119, f32[1024,128]{1,0:T(8,128)S(1)} %broadcast_in_dim.42.keep, f32[1,256]{1,0:T(1,128)S(1)} %bitcast.123, ...), custom_call_target="tpu_custom_call" | custom-call | tf_op jit(solution)/shard_map/front/pallas_call | solution.py:653
  67.8 77.2 %weights_gather.1 = (bf16[1024,128]{1,0:T(8,128)(2,1)S(1)}, bf16[1024,512]{1,0:T(8,128)(2,1)S(1)}, bf16[1024,512]{1,0:T(8,128)(2,1)S(1)}, bf16[256,1024]{1,0:T(8...) custom-call(bf16[128,128]{1,0:T(8,128)(2,1)S(1)} %copy-done.48, ...), custom_call_target="tpu_custom_call" | custom-call | tf_op jit(solution)/shard_map/weights_gather/pallas_call | solution.py:378
  145.1 2.8 multiply_convert_fusion.4
  148.2 1.5 multiply_convert_fusion.8
  149.7 3.1 core_swap.2
  152.8 1.9 maximum_select_fusion
  155.7 22.1 %while.28 = (s32[]{:T(128)}, f32[2,512,512]{2,1,0:T(8,128)}, f32[2,512]{1,0:T(2,128)S(1)}, s32[2]{0:T(128)S(1)}, s32[]{:T(128)}, /*index=5*/s32[1024]{0:T(1024)S...) while((s32[]{:T(128)}, f32[2,512,512]{2,1,0:T(8,128)}, ...), condition=%wide.region_3.4_spmd.clone, body=%wide.region_0.3_spmd.clone.sunk | while | flops 1353711616 | bytes 33200888 | solution.py:909
  157.0 2.4 fusion.135
  160.1 1.3 copy-done.67
  161.4 5.2 fusion.137
  167.9 2.4 fusion.135
  171.0 1.3 copy-done.67
  172.4 5.2 fusion.137
  177.8 1.9 fusion.44
  179.8 2.1 convolution_convert_fusion.6.refs_1_
  181.9 2.8 fusion.27
  186.9 39.6 %tp_scatter.3 = (f32[1024,256]{1,0:T(8,128)S(1)}, f32[1024,256]{1,0:T(8,128)S(1)}) custom-call(bf16[1024,1024]{1,0:T(8,128)(2,1)S(1)} %add_convert_fusion.refs_0_, bf16[1024,1024]{1,0:T(8,128)(2,1)} %convolution_convert_fusion.6.refs_1_), custom_call_target="tpu_custom_call" | custom-call | tf_op jit(solution)/shard_map/tp_scatter/pallas_call | solution.py:231
  228.3 8.9 %psum.70 = f32[1024]{0:T(1024)S(1)} all-reduce(f32[1024]{0:T(1024)S(1)} %get-tuple-element.357), channel_id=1, replica_groups=mesh['fsdp'=4,'ctx'=2,'tp'=4] {'tp'}, use_global_device_ids=true, to_apply=%region_5.6 | all-reduce | flops 1024 | bytes 8192 | tf_op jit(solution)/shard_map/psum | solution.py:919
  237.5 34.8 %tp_gather.2 = (bf16[1024,1024]{1,0:T(8,128)(2,1)S(1)}, bf16[1024,1024]{1,0:T(8,128)(2,1)S(1)}) custom-call(bf16[1024,256]{1,0:T(8,128)(2,1)S(1)} %multiply_convert_fusion.6.refs_0_, bf16[1024,256]{1,0:T(8,128)(2,1)S(1)} %bitcast.121), custom_call_target="tpu_custom_call" | custom-call | tf_op jit(solution)/shard_map/tp_gather/pallas_call | solution.py:130
  272.3 2.3 fusion.59
  275.4 2.3 convolution_convert_fusion.5.refs_0_
  277.7 3.1 multiply_convert_fusion
  280.9 1.3 copy-done.96
  282.2 3.7 convolution_convert_fusion.4.refs_1_
  285.9 35.9 %tp_scatter.4 = (f32[1024,256]{1,0:T(8,128)S(1)}, f32[1024,256]{1,0:T(8,128)S(1)}) custom-call(bf16[1024,1024]{1,0:T(8,128)(2,1)S(1)} %convolution_convert_fusion.5.refs_0_, bf16[1024,1024]{1,0:T(8,128)(2,1)} %convolution_convert_fusion.4.refs_1_), custom_call_target="tpu_custom_call" | custom-call | tf_op jit(solution)/shard_map/tp_scatter/pallas_call | solution.py:231
  323.2 8.9 %psum.71 = f32[1024]{0:T(1024)S(1)} all-reduce(f32[1024]{0:T(1024)S(1)} %get-tuple-element.298), channel_id=1, replica_groups=mesh['fsdp'=4,'ctx'=2,'tp'=4] {'tp'}, use_global_device_ids=true, to_apply=%region_7.8 | all-reduce | flops 1024 | bytes 8192 | tf_op jit(solution)/shard_map/psum | solution.py:934
  332.2 3.7 fusion.36
  335.9 30.9 %tp_gather.3 = (bf16[1024,1024]{1,0:T(8,128)(2,1)S(1)}, bf16[1024,1024]{1,0:T(8,128)(2,1)S(1)}) custom-call(bf16[1024,256]{1,0:T(8,128)(2,1)S(1)} %get-tuple-element.364.refs_0_, bf16[1024,256]{1,0:T(8,128)(2,1)S(1)} %get-tuple-element.363.refs_1_), custom_call_target="tpu_custom_call" | custom-call | tf_op jit(solution)/shard_map/tp_gather/pallas_call | solution.py:130
  366.8 3.4 fusion.29
  370.2 54.8 %while.29 = (s32[]{:T(128)}, f32[2048,128]{1,0:T(8,128)}, f32[2048,512]{1,0:T(8,128)}, f32[2,512,128]{2,1,0:T(8,128)}, s32[2]{0:T(128)S(1)}, /*index=5*/s32[]{:T...) while((s32[]{:T(128)}, f32[2048,128]{1,0:T(8,128)}, ...), condition=%wide.region_10.11_spmd.clone, body=%wide.region_8.10_spmd.clone.sunk | while | flops 3509387264 | bytes 127562688 | solution.py:977
  371.5 5.0 fusion.151
  376.6 3.9 multiply_reduce_fusion.7
  380.6 2.8 subtract_convert_fusion.2
  383.4 3.1 fusion.152
  386.4 1.4 fusion.153
  387.8 2.5 convolution_add_fusion.7
  390.3 1.8 convolution_add_fusion.8
  392.9 3.4 select_add_fusion.2
  397.5 5.0 fusion.151
  402.7 3.9 multiply_reduce_fusion.7
  406.6 2.8 subtract_convert_fusion.2
  409.4 3.1 fusion.152
  412.5 1.4 fusion.153
  413.9 2.7 convolution_add_fusion.7
  416.7 1.8 convolution_add_fusion.8
  419.2 5.6 select_add_fusion.2
  425.0 3.2 constant_dynamic-slice_fusion.refs_1_
  428.2 1.6 copy-done
  429.8 4.9 core_swap.3
  437.0 6.1 convolution_convert_fusion.1.refs_6_
  443.1 2.2 convolution_convert_fusion.7.refs_4_
  449.3 2.3 convolution_convert_fusion.9.refs_1_
  453.4 2.3 convolution_convert_fusion.8.refs_2_
  455.7 2.7 convolution_convert_fusion.2.refs_1_
  459.4 1.7 convolution_add_fusion.4
  461.9 48.5 %tp_scatter.5 = (f32[1024,256]{1,0:T(8,128)S(1)}, f32[1024,256]{1,0:T(8,128)S(1)}) custom-call(bf16[1024,1024]{1,0:T(8,128)(2,1)S(1)} %convolution_convert_fusion.3.refs_0_, bf16[1024,1024]{1,0:T(8,128)(2,1)} %convolution_convert_fusion.2.refs_1_), custom_call_target="tpu_custom_call" | custom-call | tf_op jit(solution)/shard_map/tp_scatter/pallas_call | solution.py:231
  511.4 3.9 convolution_convert_fusion.refs_7_
  515.3 1.5 multiply_reduce_fusion.4
  516.8 2.5 convolution_convert_fusion.12.refs_0_
  519.4 86.6 %grads_scatter.1 = (f32[128,128]{1,0:T(8,128)S(1)}, f32[128,512]{1,0:T(8,128)S(1)}, f32[128,512]{1,0:T(8,128)S(1)}, f32[256,128]{1,0:T(8,128)S(1)}, f32[512,128]...) custom-call(bf16[1024,128]{1,0:T(8,128)(2,1)S(1)} %convolution_convert_fusion.12.refs_0_, ...), custom_call_target="tpu_custom_call" | custom-call | tf_op jit(solution)/shard_map/grads_scatter/pallas_call | solution.py:485
  607.7 1.4 fusion.31.mix_sum
  609.4 30.5 %tail.1 = (f32[1024,256]{1,0:T(8,128)S(1)}, f32[1,256]{1,0:T(1,128)S(1)}, f32[16,256]{1,0:T(8,128)S(1)}, f32[16,256]{1,0:T(8,128)S(1)}) custom-call(f32[1024,256]{1,0:T(8,128)S(1)} %fusion.31.mix_sum, f32[1024,256]{1,0:T(8,128)S(1)} %copy-done.19, f32[2,1024,128]{2,1,0:T(8,128)S(1)} %copy-done.16, f32[2,1024,128]{2,1,0:T(8,128)} %copy-done.17, ...), custom_call_target="tpu_custom_call" | custom-call | tf_op jit(solution)/shard_map/tail/pallas_call | solution.py:794
  639.9 34.4 %all-reduce = (f32[256]{0:T(256)}, f32[16,256]{1,0:T(8,128)}, f32[16,256]{1,0:T(8,128)}, f32[128]{0:T(128)}, f32[128]{0:T(128)}, /*index=5*/f32[256]{0:T(256)}) all-reduce(f32[256]{0:T(256)S(1)} %bitcast.125, f32[16,256]{1,0:T(8,128)S(1)} %get-tuple-element.221, ...), channel_id=1, replica_groups=mesh['fsdp'=4,'ctx'=2,'tp'=4] {'fsdp','ctx'}, use_global_device_ids=true, to_apply=%region_13.14 | all-reduce | flops 8960 | bytes 71680 | tf_op jit(solution)/shard_map/psum | solution.py:1015
  (266 shorter events, 46.0 us)
Async XLA Ops:
  7.2 508.1 %all-reduce.4.cloned.1.call-start = ((), (), s32[]{:S(2)}) async-start(), calls=%async_computation | async-start | bytes 2097152 | tf_op jit(solution)/shard_map/psum | solution.py:993
  67.8 80.1 %copy-start.46 = (f32[8,1024]{1,0:T(8,128)}, f32[8,1024]{1,0:T(8,128)S(1)}, u32[]{:S(2)}) copy-start(f32[8,1024]{1,0:T(8,128)S(1)} %get-tuple-element.218.inv_in) | copy-start | bytes 98308
  67.8 80.1 %copy-start.52 = (bf16[1024,1024]{1,0:T(8,128)(2,1)}, bf16[1024,1024]{1,0:T(8,128)(2,1)S(1)}, u32[]{:S(2)}) copy-start(bf16[1024,1024]{1,0:T(8,128)(2,1)S(1)} %get-tuple-element.191) | copy-start | bytes 6291460
  145.0 2.9 copy-start.59
  145.1 2.9 copy-start.49
  145.1 32.7 %copy-start.23 = (bf16[256,1024]{1,0:T(8,128)(2,1)}, bf16[256,1024]{1,0:T(8,128)(2,1)S(1)}, u32[]{:S(2)}) copy-start(bf16[256,1024]{1,0:T(8,128)(2,1)S(1)} %get-tuple-element.188) | copy-start | bytes 1572868
  145.1 34.7 %copy-start.9 = (bf16[256,1024]{1,0:T(8,128)(2,1)}, bf16[256,1024]{1,0:T(8,128)(2,1)S(1)}, u32[]{:S(2)}) copy-start(bf16[256,1024]{1,0:T(8,128)(2,1)S(1)} %get-tuple-element.197) | copy-start | bytes 1572868
  145.1 36.8 %copy-start.57 = (bf16[1024,512]{1,0:T(8,128)(2,1)}, bf16[1024,512]{1,0:T(8,128)(2,1)S(1)}, u32[]{:S(2)}) copy-start(bf16[1024,512]{1,0:T(8,128)(2,1)S(1)} %get-tuple-element.189) | copy-start | bytes 3145732
  145.1 39.6 %copy-start.20 = (bf16[512,1024]{1,0:T(8,128)(2,1)}, bf16[512,1024]{1,0:T(8,128)(2,1)S(1)}, u32[]{:S(2)}) copy-start(bf16[512,1024]{1,0:T(8,128)(2,1)S(1)} %get-tuple-element.196) | copy-start | bytes 3145732
  145.1 3.1 copy-start.73
  145.1 3.1 copy-start.85
  145.1 3.1 copy-start.87
  152.8 2.8 copy-start.82
  186.9 40.7 %copy-start.4 = (bf16[1,1024,256]{2,1,0:T(8,128)(2,1)S(1)}, bf16[1,1024,256]{2,1,0:T(8,128)(2,1)}, u32[]{:S(2)}) copy-start(bf16[1,1024,256]{2,1,0:T(8,128)(2,1)} %param.21) | copy-start | bytes 1572868
  226.6 10.6 %copy-start.84 = (f32[256]{0:T(256)S(1)}, f32[256]{0:T(256)}, u32[]{:S(2)}) copy-start(f32[256]{0:T(256)} %param.29) | copy-start | bytes 3076
  227.6 9.9 %copy-start.8 = (bf16[1,1024,256]{2,1,0:T(8,128)(2,1)S(1)}, bf16[1,1024,256]{2,1,0:T(8,128)(2,1)}, u32[]{:S(2)}) copy-start(bf16[1,1024,256]{2,1,0:T(8,128)(2,1)} %param.23) | copy-start | bytes 1572868
  228.3 46.4 %copy-start.71 = (f32[1024,256]{1,0:T(8,128)}, f32[1024,256]{1,0:T(8,128)S(1)}, u32[]{:S(2)}) copy-start(f32[1024,256]{1,0:T(8,128)S(1)} %get-tuple-element.358) | copy-start | bytes 3145732
  237.2 35.0 %copy-start.89 = (bf16[1024,1024]{1,0:T(8,128)(2,1)S(1)}, bf16[1024,1024]{1,0:T(8,128)(2,1)}, u32[]{:S(2)}) copy-start(bf16[1024,1024]{1,0:T(8,128)(2,1)} %get-tuple-element.201) | copy-start | bytes 6291460
  272.2 2.4 copy-start.56
  272.3 5.5 copy-start.54
  272.3 3.1 copy-start.90
  274.6 3.1 copy-start.93
  285.9 36.9 %copy-start.72 = (f32[1024,256]{1,0:T(8,128)S(1)}, f32[1024,256]{1,0:T(8,128)}, u32[]{:S(2)}) copy-start(f32[1024,256]{1,0:T(8,128)} %copy-done.71) | copy-start | bytes 3145732
  332.2 34.6 %copy-start.21 = (bf16[512,1024]{1,0:T(8,128)(2,1)S(1)}, bf16[512,1024]{1,0:T(8,128)(2,1)}, u32[]{:S(2)}) copy-start(bf16[512,1024]{1,0:T(8,128)(2,1)} %copy-done.20) | copy-start | bytes 3145732
  332.2 34.6 %copy-start.92 = (f32[2,512,512]{2,1,0:T(8,128)S(1)}, f32[2,512,512]{2,1,0:T(8,128)}, u32[]{:S(2)}) copy-start(f32[2,512,512]{2,1,0:T(8,128)} %get-tuple-element.195) | copy-start | bytes 6291460
  332.2 34.6 %copy-start.97 = (f32[1024,512]{1,0:T(8,128)S(1)}, f32[1024,512]{1,0:T(8,128)}, u32[]{:S(2)}) copy-start(f32[1024,512]{1,0:T(8,128)} %get-tuple-element.378) | copy-start | bytes 6291460
  366.8 3.4 copy-start.1
  366.8 3.4 copy-start.68
  376.6 3.9 copy-start.66
  380.6 2.8 copy-start.61
  383.4 3.1 copy-start.63
  387.8 2.5 copy-start.64
  387.8 4.3 copy-start.77
  390.3 2.6 copy-start.62
  402.7 3.9 copy-start.66
  406.6 2.8 copy-start.61
  409.4 3.1 copy-start.63
  413.9 2.8 copy-start.64
  413.9 4.6 copy-start.77
  416.7 2.6 copy-start.62
  425.0 3.2 copy-start.69
  429.8 6.3 copy-start.70
  437.0 6.1 copy-start.2
  437.0 6.1 copy-start.79
  443.1 2.3 copy-start.24
  443.1 3.0 copy-start.65
  445.3 2.3 copy-start.80
  449.3 2.3 copy-start.60
  453.4 2.3 copy-start.58
  461.1 50.3 %copy-start.94 = (f32[1024,1024]{1,0:T(8,128)S(1)}, f32[1024,1024]{1,0:T(8,128)}, u32[]{:S(2)}) copy-start(f32[1024,1024]{1,0:T(8,128)} %copy-done.93) | copy-start | bytes 12582916
  461.9 49.5 %copy-start.55 = (bf16[1024,1024]{1,0:T(8,128)(2,1)S(1)}, bf16[1024,1024]{1,0:T(8,128)(2,1)}, u32[]{:S(2)}) copy-start(bf16[1024,1024]{1,0:T(8,128)(2,1)} %copy-done.54) | copy-start | bytes 6291460
  511.4 3.9 copy-start.13
  511.4 3.9 copy-start.81
  511.4 3.9 copy-start.86
  511.4 3.9 copy-start.88
  516.8 2.5 copy-start.11
  516.8 2.5 copy-start.12
  519.4 88.3 %copy-start.14 = (f32[1024,256]{1,0:T(8,128)S(1)}, f32[1024,256]{1,0:T(8,128)}, u32[]{:S(2)}) copy-start(f32[1024,256]{1,0:T(8,128)} %copy-done.13) | copy-start | bytes 3145732
  519.4 88.3 %copy-start.76 = (f32[1024,256]{1,0:T(8,128)S(1)}, f32[1024,256]{1,0:T(8,128)}, u32[]{:S(2)}) copy-start(f32[1024,256]{1,0:T(8,128)} %convolution_add_fusion.4) | copy-start | bytes 3145732
  639.9 35.4 %copy-start.45 = (f32[128,128]{1,0:T(8,128)S(1)}, f32[128,128]{1,0:T(8,128)}, u32[]{:S(2)}) copy-start(f32[128,128]{1,0:T(8,128)} %copy-done.44) | copy-start | bytes 196612
  639.9 36.7 %copy-start.30 = (f32[128,512]{1,0:T(8,128)S(1)}, f32[128,512]{1,0:T(8,128)}, u32[]{:S(2)}) copy-start(f32[128,512]{1,0:T(8,128)} %copy-done.29) | copy-start | bytes 786436
  639.9 37.4 %copy-start.37 = (f32[256,128]{1,0:T(8,128)S(1)}, f32[256,128]{1,0:T(8,128)}, u32[]{:S(2)}) copy-start(f32[256,128]{1,0:T(8,128)} %copy-done.36) | copy-start | bytes 393220
  674.3 5.0 copy-start.28
  675.3 4.9 copy-start.26
  (42 other events, 54.3 us)
Sparse Core Ops, SparseCore 0:
  437.1 60.3 all-reduce.3
